TPU v7x, 256 devices: a whole 4x4x8 slice. The times are simulated.
256 devices in a mesh: blk: 64 (over x, z, core), pair: 4 (over y).
Axes of the slice: x: 4, y: 4, z: 8, core: 2. Of those that a mesh axis runs over, the one named last changes fastest.
Arguments:
- records: bfloat16 [64, 8192, 2048], P('blk', 'pair'), may hold values from -100 to 100
- offsets: int32 [2], replicated, may hold values from 1 to 15, as said below
- source_side: int32 [64, 2], P('blk'), may hold values from 0 to 1
Outputs:
- first_side: bfloat16 [64, 2, 32, 128, 128], P('blk', None, 'pair')
- second_side: bfloat16 [64, 2, 32, 128, 128], P('blk', None, 'pair')
Inputs may be any that keep to these rules, and one draw needn't show every extreme that they name: `offsets`: distinct and increasing; the last one is 15.
All inputs are finite; a program needn't handle non-finite values.
Results may differ from a plain program's by a relative error of at most 0.012.
Values may be sent and summed in bfloat16 or wider, within the bound.
A program may use at most 128 MiB of HBM per device.

v0:
```python
import math

import jax
import jax.numpy as jnp
from jax import lax
from jax.sharding import PartitionSpec as P

BLOCK_CH = 128
BINS = 128
SAMPLES = 2048
FIRST_BIN = 4
LAGS = 32


def as_sent(value):
    return jax.tree.map(lambda a: a.astype(jnp.bfloat16) if a.dtype == jnp.float32 else a, value)


def shifted(value, axis, steps):
    count = lax.axis_size(axis)
    leading, last = (max(0, -steps), min(count, count - steps))
    return lax.ppermute(value, axis, [(source, source + steps) for source in range(leading, last)])


def cut_along(value, dim, count):
    dims = value.shape
    tiles = value.reshape(*dims[:dim], count, dims[dim] // count, *dims[dim + 1 :])
    return jnp.moveaxis(tiles, dim, 0)


def sum_at_owner(value, axis, dim):
    tiles = cut_along(value, dim, lax.axis_size(axis))
    arrived = lax.all_to_all(tiles, axis, split_axis=0, concat_axis=0, tiled=True)
    return arrived.astype(jnp.float32).sum(axis=0)


def fourier_table():
    sample_index = jnp.arange(SAMPLES, dtype=jnp.int32)
    bin_index = FIRST_BIN + jnp.arange(BINS, dtype=jnp.int32)
    phase_index = sample_index[:, None] * bin_index[None, :] % SAMPLES
    angles = 2.0 * math.pi / SAMPLES * phase_index.astype(jnp.float32)
    hann_taper = 0.5 - 0.5 * jnp.cos(2.0 * math.pi / SAMPLES * sample_index.astype(jnp.float32))
    return jnp.stack(
        (hann_taper[:, None] * jnp.cos(angles), -hann_taper[:, None] * jnp.sin(angles)), axis=-1
    )


def shift_ahead(distance):
    return lambda block: jax.tree.map(
        lambda part, own: part.astype(own.dtype), shifted(as_sent(block), "blk", -distance), block
    )


def shift_behind(distance):
    return lambda block: jax.tree.map(
        lambda part, own: part.astype(own.dtype), shifted(as_sent(block), "blk", distance), block
    )


def local(records, offsets, source_side):
    seg_local = records.shape[0]
    local_blocks = records.shape[1] // BLOCK_CH
    table_full = fourier_table()
    table_high = lax.optimization_barrier(table_full.astype(jnp.bfloat16))
    table_low = (table_full - table_high.astype(jnp.float32)).astype(jnp.bfloat16)
    traces = records.reshape(seg_local, local_blocks, BLOCK_CH, SAMPLES)
    spectrum = jnp.einsum("sbcn,nfr->bfsrc", traces, table_high, preferred_element_type=jnp.float32)
    spectrum = spectrum + jnp.einsum(
        "sbcn,nfr->bfsrc", traces, table_low, preferred_element_type=jnp.float32
    )
    band_power = jnp.sum(spectrum * spectrum, axis=3)
    band_level = jnp.mean(band_power, axis=-1)
    whiten_scale = 1.0 / jnp.sqrt(band_level + 1e-05)
    whitened = (spectrum * whiten_scale[:, :, :, None, None]).astype(jnp.bfloat16)
    regrouped = lax.all_to_all(
        lax.all_to_all(whitened, "pair", split_axis=1, concat_axis=0, tiled=True),
        "blk",
        split_axis=0,
        concat_axis=2,
        tiled=True,
    )
    own_block = regrouped[0]
    bin_local = own_block.shape[0]
    seg_total = own_block.shape[1]
    offset_total = offsets.shape[0]
    group_size = lax.axis_size("blk")
    window_size = min(16, group_size)
    ahead_list = [shift_ahead(distance) for distance in range(1, window_size)]
    partners = jnp.stack(
        [lax.switch(offsets[slot] - 1, ahead_list, own_block) for slot in range(offset_total)]
    )
    reverse_side = (source_side[0] == 1)[:, None, None, None, None]
    own_many = jnp.broadcast_to(own_block[None], partners.shape)
    source = jnp.where(reverse_side, partners, own_many)
    receiver = jnp.where(reverse_side, own_many, partners)
    left_side = source.reshape(offset_total, bin_local, 2 * seg_total, BLOCK_CH)
    rotated = jnp.stack((receiver[:, :, :, 1], -receiver[:, :, :, 0]), axis=3)
    right_side = jnp.stack((receiver, rotated), axis=4).reshape(
        offset_total, bin_local, 2 * seg_total, 2, BLOCK_CH
    )
    cross = jnp.einsum(
        "kfsc,kfsrd->kfrcd", left_side, right_side, preferred_element_type=jnp.float32
    )
    cross_rows = cross.reshape(offset_total, 2 * bin_local, BLOCK_CH * BLOCK_CH)
    pair_index = lax.axis_index("pair")
    lag_index = jnp.arange(LAGS, dtype=jnp.int32) - LAGS // 2
    bin_index = FIRST_BIN + pair_index * bin_local + jnp.arange(bin_local, dtype=jnp.int32)
    phase_index = lag_index[:, None] * bin_index[None, :] % SAMPLES
    angles = 2.0 * math.pi / SAMPLES * phase_index.astype(jnp.float32)
    normalizer = 1.0 / math.sqrt(seg_total * BINS)
    lag_table = (jnp.stack((jnp.cos(angles), -jnp.sin(angles)), axis=-1) * normalizer).reshape(
        LAGS, 2 * bin_local
    )
    summed = sum_at_owner(
        jnp.einsum("lq,kqx->lkx", lag_table, cross_rows, preferred_element_type=jnp.float32).astype(
            jnp.bfloat16
        ),
        "pair",
        0,
    )
    lag_local = summed.shape[0]
    first_local = (
        summed.astype(jnp.bfloat16)
        .transpose(1, 0, 2)
        .reshape(offset_total, lag_local, BLOCK_CH, BLOCK_CH)
    )
    behind_list = [shift_behind(distance) for distance in range(1, window_size)]
    returned = jnp.stack(
        [
            lax.switch(offsets[slot] - 1, behind_list, first_local[slot])
            for slot in range(offset_total)
        ]
    )
    return (first_local[None], returned[None])


def solution(mesh):
    placed = (P("blk", "pair", None), P(), P("blk", None))
    return jax.shard_map(
        local,
        mesh=mesh,
        in_specs=placed,
        out_specs=(P("blk", None, "pair", None, None), P("blk", None, "pair", None, None)),
        check_vma=False,
    )
```

profile of v0, /device:TPU:2, one launch (start us, length us, event | category | flops | bytes accessed | tf_op | source)
XLA Modules:
  0.0 248.9 jit_solution(16565884516497682835)
XLA Ops:
  0.6 0.1 multiply_subtract_fusion
  0.7 4.2 %cosine_multiply_fusion = (f32[2048,128,1]{1,0,2:T(8,128)S(1)}, f32[2048,128,1]{1,0,2:T(8,128)S(1)}) fusion(s32[128]{0:T(128)S(1)} %iota_add_fusion, f32[2048]{0:T(1024)S(1)} %get-tuple-element.202, f32[2048]{0:T(1024)S(1)} %get-tuple-element.203), kind=kLoop, calls=%fused_computation.67 | loop fusion | flops 4194304 | bytes 2114048 | tf_op jit(solution)/shard_map/mul | solution.py:44
  4.9 0.0 slice-start
  4.9 0.2 fusion.15
  5.0 0.0 slice-start.1
  5.1 6.0 %fusion.21 = f32[128,2,16,128]{0,3,2,1:T(8,128)S(1)} fusion(bf16[16,128,2048,1]{2,1,0,3:T(8,128)(2,1)} %bitcast.238, bf16[2048,128,2]{1,0,2:T(8,128)(2,1)S(1)} %fusion.15), kind=kOutput, calls=%fused_computation.61 | convolution fusion | flops 2147483648 | bytes 11534336 | tf_op jit(solution)/shard_map/sbcn,nfr->bfsrc/dot_general | solution.py:67
  11.1 0.0 slice-done
  11.1 0.0 slice-done.1
  11.1 2.6 %fusion.12 = (f32[16,128]{1,0:T(8,128)S(1)}, f32[128,2,16,128]{0,3,2,1:T(8,128)S(1)}) fusion(f32[128,2,16,128]{0,3,2,1:T(8,128)S(1)} %fusion.21, bf16[16,128,2048,1]{2,1,0,3:T(8,128)(2,1)S(1)} %bitcast.241, bf16[2048,128,2]{1,0,2:T(8,128)(2,1)S(1)} %fusion.15, f32[2048,128,1]{1,0,2:T(8,128)S(1)} %get-tuple-element.197, ...), kind=kOutput, calls=%fused_computation.47 | convolution fusion | flops 2151151616 | bytes 15736832 | tf_op jit(solution)/shard_map/sbcn,nfr->bfsrc/dot_general | solution.py:68
  13.7 0.2 fusion.13
  13.9 1.0 copy.119
  14.9 19.4 %all_to_all.38 = bf16[16,128,1,2,128]{4,0,3,2,1:T(8,128)(2,1)S(1)} all-to-all(bf16[16,128,1,2,128]{4,0,3,2,1:T(8,128)(2,1)S(1)} %copy.119), channel_id=1, replica_groups=mesh['blk'=64,'pair'=4] {'pair'}, dimensions={1} | all-to-all | bytes 2097152 | tf_op jit(solution)/shard_map/all_to_all | solution.py:76
  34.3 0.4 copy.120
  34.7 0.0 copy-start.2
  34.7 0.0 copy-start.3
  34.7 1.2 copy.121
  35.9 12.0 %all-to-all-start.1 = ((bf16[64,32,1,2,128]{4,1,3,2,0:T(8,128)(2,1)}), bf16[64,32,1,2,128]{4,1,3,2,0:T(8,128)(2,1)S(1)}, u32[]{:S(2)}, u32[]{:S(2)}) async-start(bf16[64,32,1,2,128]{4,1,3,2,0:T(8,128)(2,1)} %bitcast.75), calls=%async_computation.1 | async-start | bytes 2097152 | tf_op jit(solution)/shard_map/all_to_all | solution.py:75
  47.9 0.0 copy-done.2
  47.9 0.6 fusion.35
  49.8 0.2 fusion.30
  50.0 0.1 copy.118
  50.1 0.0 copy-done.3
  50.1 24.9 %all-to-all-done.1 = bf16[64,32,1,2,128]{4,1,3,2,0:T(8,128)(2,1)S(1)} async-done(((bf16[64,32,1,2,128]{4,1,3,2,0:T(8,128)(2,1)}), bf16[64,32,1,2,128]{4,1,3,2,0:T(8,128)(2,1)S(1)}, u32[]{:S(2)}, u32[]{:S(2)}) %all-to-all-start.1) | async-done | bytes 1048608 | tf_op jit(solution)/shard_map/all_to_all | solution.py:75
  75.0 1.7 copy.122
  76.7 1.4 copy.160
  78.1 2.1 copy.123
  80.2 37.9 %conditional.4 = (bf16[32,64,2,128]{3,2,1,0:T(2,128)(2,1)}) conditional(s32[]{:T(128)} %bitcast.79, bf16[32,64,2,128]{3,2,1,0:T(2,128)(2,1)} %copy.123, bf16[32,64,2,128]{3,2,1,0:T(2,128)(2,1)} %copy.123, bf16[32,64,2,128]{3,2,1,0:T(2,128)(2,1)} %copy.123, bf16[32,64,2,128]{3,2,1,0:T(2,128)(2,1)} %copy.123, ...), branch_computations={%region_1.2_spmd, %region_2.3_spmd, %region_3.4_spmd, %region_4.5_... | conditional | bytes 4194352 | solution.py:90
  80.2 4.7 %collective-permute-start.11 = (bf16[32,64,2,128]{3,2,1,0:T(2,128)(2,1)}, bf16[32,64,2,128]{3,2,1,0:T(2,128)(2,1)}, u32[]{:S(2)}, u32[]{:S(2)}) collective-permute-start(bf16[32,64,2,128]{3,2,1,0:T(2,128)(2,1)} %param.11), channel_id=1, source_target_pairs={{48,0},{52,4},{56,8},{60,12},{64,16},{68,20},{72,24},{76,28},{80,3... | collective-permute-start | bytes 3145736 | tf_op jit(solution)/shard_map/cond/branch_11_fun/ppermute | solution.py:22
  84.9 33.1 %collective-permute-done.11 = bf16[32,64,2,128]{3,2,1,0:T(2,128)(2,1)} collective-permute-done((bf16[32,64,2,128]{3,2,1,0:T(2,128)(2,1)}, bf16[32,64,2,128]{3,2,1,0:T(2,128)(2,1)}, u32[]{:S(2)}, u32[]{:S(2)}) %collective-permute-start.11) | collective-permute-done | bytes 1048608 | tf_op jit(solution)/shard_map/cond/branch_11_fun/ppermute | solution.py:22
  118.1 2.4 copy.210
  120.5 2.3 copy.155
  122.8 28.2 %conditional.5 = (bf16[32,64,2,128]{3,2,1,0:T(2,128)(2,1)}) conditional(s32[]{:T(128)} %bitcast.84, bf16[32,64,2,128]{3,2,1,0:T(2,128)(2,1)} %copy.123, bf16[32,64,2,128]{3,2,1,0:T(2,128)(2,1)} %copy.123, bf16[32,64,2,128]{3,2,1,0:T(2,128)(2,1)} %copy.123, bf16[32,64,2,128]{3,2,1,0:T(2,128)(2,1)} %copy.123, ...), branch_computations={%region_16.17_spmd, %region_17.18_spmd, %region_18.19_spmd, %regio... | conditional | bytes 4194352 | solution.py:90
  122.8 1.9 collective-permute-start.29
  124.7 26.2 %collective-permute-done.29 = bf16[32,64,2,128]{3,2,1,0:T(2,128)(2,1)} collective-permute-done((bf16[32,64,2,128]{3,2,1,0:T(2,128)(2,1)}, bf16[32,64,2,128]{3,2,1,0:T(2,128)(2,1)}, u32[]{:S(2)}, u32[]{:S(2)}) %collective-permute-start.29) | collective-permute-done | bytes 1048608 | tf_op jit(solution)/shard_map/cond/branch_14_fun/ppermute | solution.py:22
  150.9 3.4 %copy.209 = bf16[32,64,2,128]{3,0,2,1:T(8,128)(2,1)} copy(bf16[32,64,2,128]{3,2,1,0:T(2,128)(2,1)} %get-tuple-element.235) | data formatting | bytes 2097152 | tf_op jit(solution)/shard_map/cond | solution.py:90
  154.4 2.3 copy.156
  156.7 1.5 maximum_select_fusion.1
  158.2 0.2 fusion.34
  158.4 0.2 pad_maximum_fusion.1
  158.6 3.0 %copy.159 = bf16[2,32,128,1,128]{2,4,3,1,0:T(8,128)(2,1)} copy(bf16[2,32,128,1,128]{4,1,2,0,3:T(8,128)(2,1)S(1)} %bitcast.202) | data formatting | bytes 4194304 | tf_op jit(solution)/shard_map/stack | solution.py:98
  161.6 0.0 copy-start
  161.6 0.0 copy-start.1
  161.6 2.3 maximum_select_fusion
  163.9 0.2 copy-done
  164.1 0.3 copy-done.1
  164.4 4.9 %fusion.5 = bf16[2,32,2,128,128]{3,4,2,1,0:T(8,128)(2,1)} fusion(bf16[2,32,128,1,128]{2,4,3,1,0:T(8,128)(2,1)S(1)} %copy-done, bf16[2,32,128,1,128]{2,4,3,1,0:T(8,128)(2,1)S(1)} %maximum_select_fusion, bf16[1,32,128,128]{3,2,1,0:T(8,128)(2,1)} %bitcast.90, bf16[1,32,128,128]{3,2,1,0:T(8,128)(2,1)} %bitcast.89, pred[2]{0:T(512)(128)(4,1)S(1)} %compare_bitcast_fusion, ...), kind=kOutput, calls=%fused_computation.36 | convolution fusion | flops 541065216 | bytes 11534338 | tf_op jit(solution)/shard_map/kfsc,kfsrd->kfrcd/dot_general | solution.py:101
  169.2 6.4 %copy.161 = bf16[2,32,2,128,128]{4,3,2,1,0:T(8,128)(2,1)} copy(bf16[2,32,2,128,128]{3,4,2,1,0:T(8,128)(2,1)} %fusion.5) | data formatting | bytes 8388608 | tf_op jit(solution)/shard_map/kfsc,kfsrd->kfrcd/transpose | solution.py:101
  175.6 7.3 %reshape.416 = bf16[2,64,16384]{2,1,0:T(8,128)(2,1)} reshape(bf16[2,32,2,128,128]{4,3,2,1,0:T(8,128)(2,1)} %copy.161) | data formatting | bytes 8388608 | tf_op jit(solution)/shard_map/reshape | solution.py:104
  182.9 2.9 %fusion = bf16[4,8,2,16384]{3,1,0,2:T(8,128)(2,1)S(1)} fusion(bf16[32,64,1]{0,1,2:T(8,128)(2,1)S(1)} %bitcast.237, bf16[2,64,16384]{2,1,0:T(8,128)(2,1)} %reshape.416), kind=kOutput, calls=%fused_computation.31 | convolution fusion | flops 134217728 | bytes 6295552 | tf_op jit(solution)/shard_map/lq,kqx->lkx/dot_general | solution.py:115
  185.8 0.1 copy.163
  186.0 29.1 %all_to_all.39 = bf16[4,8,2,16384]{3,1,2,0:T(8,128)(2,1)S(1)} all-to-all(bf16[4,8,2,16384]{3,1,2,0:T(8,128)(2,1)S(1)} %copy.163), channel_id=1, replica_groups=mesh['blk'=64,'pair'=4] {'pair'}, dimensions={0} | all-to-all | bytes 4194304 | tf_op jit(solution)/shard_map/all_to_all | solution.py:33
  215.1 0.6 reduce_sum.26
  215.8 13.5 %conditional.6 = (bf16[1,8,128,128]{3,2,1,0:T(8,128)(2,1)S(1)}) conditional(s32[]{:T(128)} %bitcast.79, bf16[2,8,16384]{2,1,0:T(8,128)(2,1)S(1)} %bitcast.167, bf16[2,8,16384]{2,1,0:T(8,128)(2,1)S(1)} %bitcast.168, bf16[2,8,16384]{2,1,0:T(8,128)(2,1)S(1)} %bitcast.169, ...), branch_computations={%region_32.33_spmd, %region_33.34_spmd, %region_34.35_spmd, %regio... | conditional | bytes 2097200 | solution.py:130
  215.8 6.8 %collective-permute-start.41 = (bf16[8,128,128]{2,0,1:T(8,128)(2,1)S(1)}, bf16[8,128,128]{2,0,1:T(8,128)(2,1)S(1)}, u32[]{:S(2)}, u32[]{:S(2)}) collective-permute-start(bf16[8,128,128]{2,0,1:T(8,128)(2,1)S(1)} %slice_bitcast_fusion.11), channel_id=1, source_target_pairs={{0,48},{4,52},{8,56},{12,60},{16,64},{20,68},{24,72},{28,76},{32,8... | collective-permute-start | bytes 786440 | tf_op jit(solution)/shard_map/cond/branch_11_fun/ppermute | solution.py:22
  222.6 6.6 %collective-permute-done.41 = bf16[8,128,128]{2,0,1:T(8,128)(2,1)S(1)} collective-permute-done((bf16[8,128,128]{2,0,1:T(8,128)(2,1)S(1)}, bf16[8,128,128]{2,0,1:T(8,128)(2,1)S(1)}, u32[]{:S(2)}, u32[]{:S(2)}) %collective-permute-start.41) | collective-permute-done | bytes 262176 | tf_op jit(solution)/shard_map/cond/branch_11_fun/ppermute | solution.py:22
  229.2 18.0 %conditional.7 = (bf16[1,8,128,128]{3,2,1,0:T(8,128)(2,1)S(1)}) conditional(s32[]{:T(128)} %bitcast.84, bf16[2,8,16384]{2,1,0:T(8,128)(2,1)S(1)} %bitcast.182, bf16[2,8,16384]{2,1,0:T(8,128)(2,1)S(1)} %bitcast.183, bf16[2,8,16384]{2,1,0:T(8,128)(2,1)S(1)} %bitcast.184, ...), branch_computations={%region_47.48_spmd, %region_48.49_spmd, %region_49.50_spmd, %regio... | conditional | bytes 2097200 | solution.py:130
  229.3 14.0 %collective-permute-start.59 = (bf16[8,128,128]{2,0,1:T(8,128)(2,1)S(1)}, bf16[8,128,128]{2,0,1:T(8,128)(2,1)S(1)}, u32[]{:S(2)}, u32[]{:S(2)}) collective-permute-start(bf16[8,128,128]{2,0,1:T(8,128)(2,1)S(1)} %slice_bitcast_fusion.29), channel_id=1, source_target_pairs={{0,60},{4,64},{8,68},{12,72},{16,76},{20,80},{24,84},{28,88},{32,9... | collective-permute-start | bytes 786440 | tf_op jit(solution)/shard_map/cond/branch_14_fun/ppermute | solution.py:22
  243.3 3.9 %collective-permute-done.59 = bf16[8,128,128]{2,0,1:T(8,128)(2,1)S(1)} collective-permute-done((bf16[8,128,128]{2,0,1:T(8,128)(2,1)S(1)}, bf16[8,128,128]{2,0,1:T(8,128)(2,1)S(1)}, u32[]{:S(2)}, u32[]{:S(2)}) %collective-permute-start.59) | collective-permute-done | bytes 262176 | tf_op jit(solution)/shard_map/cond/branch_14_fun/ppermute | solution.py:22
  247.2 0.9 copy.211
  248.1 0.8 maximum_bitcast_fusion
  (10 shorter events, 0.1 us)
Async XLA Ops:
  4.9 6.2 %slice-start = ((s8[8388608]{0:T(1024)(128)(4,1)}), s8[4194304]{0:T(1024)(128)(4,1)S(1)}, s32[]{:S(2)}) async-start(s8[8388608]{0:T(1024)(128)(4,1)} %bitcast.239), calls=%async_computation.3 | async-start | bytes 8388608
  5.0 6.0 %slice-start.1 = ((s8[8388608]{0:T(1024)(128)(4,1)}), s8[4194304]{0:T(1024)(128)(4,1)S(1)}, s32[]{:S(2)}) async-start(s8[8388608]{0:T(1024)(128)(4,1)} %bitcast.239), calls=%async_computation.4 | async-start | bytes 8388608
  34.7 13.2 %copy-start.2 = (s32[2]{0:T(128)S(1)}, s32[2]{0:T(128)}, u32[]{:S(2)}) copy-start(s32[2]{0:T(128)} %param.64) | copy-start | bytes 28
  34.7 15.4 %copy-start.3 = (s32[1,2]{1,0:T(1,128)S(1)}, s32[1,2]{1,0:T(1,128)}, u32[]{:S(2)}) copy-start(s32[1,2]{1,0:T(1,128)} %param.65) | copy-start | bytes 28
  35.9 39.2 %all-to-all-start.1 = ((bf16[64,32,1,2,128]{4,1,3,2,0:T(8,128)(2,1)}), bf16[64,32,1,2,128]{4,1,3,2,0:T(8,128)(2,1)S(1)}, u32[]{:S(2)}, u32[]{:S(2)}) async-start(bf16[64,32,1,2,128]{4,1,3,2,0:T(8,128)(2,1)} %bitcast.75), calls=%async_computation.1 | async-start | bytes 2097152 | tf_op jit(solution)/shard_map/all_to_all | solution.py:75
  80.2 37.9 %collective-permute-start.11 = (bf16[32,64,2,128]{3,2,1,0:T(2,128)(2,1)}, bf16[32,64,2,128]{3,2,1,0:T(2,128)(2,1)}, u32[]{:S(2)}, u32[]{:S(2)}) collective-permute-start(bf16[32,64,2,128]{3,2,1,0:T(2,128)(2,1)} %param.11), channel_id=1, source_target_pairs={{48,0},{52,4},{56,8},{60,12},{64,16},{68,20},{72,24},{76,28},{80,3... | collective-permute-start | bytes 3145736 | tf_op jit(solution)/shard_map/cond/branch_11_fun/ppermute | solution.py:22
  122.8 28.2 %collective-permute-start.29 = (bf16[32,64,2,128]{3,2,1,0:T(2,128)(2,1)}, bf16[32,64,2,128]{3,2,1,0:T(2,128)(2,1)}, u32[]{:S(2)}, u32[]{:S(2)}) collective-permute-start(bf16[32,64,2,128]{3,2,1,0:T(2,128)(2,1)} %param.29), channel_id=1, source_target_pairs={{60,0},{64,4},{68,8},{72,12},{76,16},{80,20},{84,24},{88,28},{92,3... | collective-permute-start | bytes 3145736 | tf_op jit(solution)/shard_map/cond/branch_14_fun/ppermute | solution.py:22
  161.6 2.5 %copy-start = (bf16[2,32,128,1,128]{2,4,3,1,0:T(8,128)(2,1)S(1)}, bf16[2,32,128,1,128]{2,4,3,1,0:T(8,128)(2,1)}, u32[]{:S(2)}) copy-start(bf16[2,32,128,1,128]{2,4,3,1,0:T(8,128)(2,1)} %copy.159) | copy-start | bytes 6291460
  161.6 2.8 %copy-start.1 = (bf16[32,128,128]{2,1,0:T(8,128)(2,1)S(1)}, bf16[32,128,128]{2,1,0:T(8,128)(2,1)}, u32[]{:S(2)}) copy-start(bf16[32,128,128]{2,1,0:T(8,128)(2,1)} %copy.160) | copy-start | bytes 3145732
  215.8 13.3 %collective-permute-start.41 = (bf16[8,128,128]{2,0,1:T(8,128)(2,1)S(1)}, bf16[8,128,128]{2,0,1:T(8,128)(2,1)S(1)}, u32[]{:S(2)}, u32[]{:S(2)}) collective-permute-start(bf16[8,128,128]{2,0,1:T(8,128)(2,1)S(1)} %slice_bitcast_fusion.11), channel_id=1, source_target_pairs={{0,48},{4,52},{8,56},{12,60},{16,64},{20,68},{24,72},{28,76},{32,8... | collective-permute-start | bytes 786440 | tf_op jit(solution)/shard_map/cond/branch_11_fun/ppermute | solution.py:22
  229.3 17.8 %collective-permute-start.59 = (bf16[8,128,128]{2,0,1:T(8,128)(2,1)S(1)}, bf16[8,128,128]{2,0,1:T(8,128)(2,1)S(1)}, u32[]{:S(2)}, u32[]{:S(2)}) collective-permute-start(bf16[8,128,128]{2,0,1:T(8,128)(2,1)S(1)} %slice_bitcast_fusion.29), channel_id=1, source_target_pairs={{0,60},{4,64},{8,68},{12,72},{16,76},{20,80},{24,84},{28,88},{32,9... | collective-permute-start | bytes 786440 | tf_op jit(solution)/shard_map/cond/branch_14_fun/ppermute | solution.py:22
where the time goes:
time: 254 us; the launch traced here: 249 us
  waiting for transfers between devices  94.7 us (37%)
  blocking collectives  48.5 us (19%)
  starting transfers between devices  39.4 us (16%)
  local copies, waits for them, and re-layouts  37.1 us (15%)
  matrix products  16.4 us (6%)
  other arithmetic  10.5 us (4%)
    ppermute x4, waiting for transfers between devices, shifted(): lax.ppermute(value, axis, [(source, source + steps) for source in range(l...  69.8 us
    all_to_all x1, blocking collectives, sum_at_owner(): lax.all_to_all(tiles, axis, split_axis=0, concat_axis=0, tiled=True)  29.1 us
    ppermute x4, starting transfers between devices, shifted(): lax.ppermute(value, axis, [(source, source + steps) for source in range(l...  27.3 us
    all_to_all x1, waiting for transfers between devices, local(): lax.all_to_all(lax.all_to_all(whitened, 'pair', split_axis=1, concat_axis...  24.9 us
    all_to_all x1, blocking collectives, local(): lax.all_to_all(whitened, 'pair', split_axis=1, concat_axis=0, tiled=True)  19.4 us
    all_to_all x1, starting transfers between devices, local(): lax.all_to_all(lax.all_to_all(whitened, 'pair', split_axis=1, concat_axis...  12 us
    reshape x1, local copies, waits for them, and re-layouts, local(): cross_rows = cross.reshape(offset_total, 2 * bin_local, BLOCK_CH * BLOCK_CH)  7.3 us
    transpose x1, local copies, waits for them, and re-layouts, local(): jnp.einsum('kfsc,kfsrd->kfrcd', left_side, right_side, preferred_element_...  6.38 us
  transfers between devices with their start and end apart: 5, of which 5 were waited for; matrix products, arithmetic and copies ran while one was open for 0% of the time, Pallas kernels for 0%

commit v1 on v0

v1 whole, which is shorter than its diff:
```python
import functools
import math

import jax
import jax.numpy as jnp
import numpy as np
from jax import lax
from jax.experimental import pallas as pl
from jax.experimental.pallas import tpu as pltpu
from jax.sharding import PartitionSpec as P

BLOCK_CH = 128
BINS = 128
SAMPLES = 2048
FIRST_BIN = 4
LAGS = 32
SEGMENTS = 64
BLOCKS = 64
LAST_OFFSET = 15
PAIRS = 4
BIN_LOCAL = BINS // PAIRS
ROWS = 2 * BIN_LOCAL
LAG_LOCAL = LAGS // PAIRS
LOCAL_BLOCKS = BLOCKS // PAIRS
GROUP = 2
GROUPS = LOCAL_BLOCKS // GROUP
TILE = 16
BF16 = jnp.bfloat16
F32 = jnp.float32
MESH = pl.DeviceIdType.MESH


def fourier_rows():
    n = np.arange(SAMPLES, dtype=np.int64)
    k = FIRST_BIN + np.arange(BINS, dtype=np.int64)
    angles = 2.0 * math.pi / SAMPLES * (k[:, None] * n[None, :] % SAMPLES).astype(np.float64)
    taper = 0.5 - 0.5 * np.cos(2.0 * math.pi / SAMPLES * n.astype(np.float64))
    table = np.stack((taper * np.cos(angles), -taper * np.sin(angles)))
    table = table.reshape(2, PAIRS, BIN_LOCAL, SAMPLES).transpose(1, 0, 2, 3).reshape(2 * BINS, SAMPLES)
    high = table.astype(BF16)
    low = (table - high.astype(np.float64)).astype(BF16)
    return np.concatenate((high, low), axis=0)


def lag_rows():
    lag = np.arange(LAGS, dtype=np.int64) - LAGS // 2
    k = FIRST_BIN + np.arange(BINS, dtype=np.int64)
    angles = 2.0 * math.pi / SAMPLES * (lag[:, None] * k[None, :] % SAMPLES).astype(np.float64)
    table = np.stack((np.cos(angles), -np.sin(angles))) / math.sqrt(SEGMENTS * BINS)
    table = table.reshape(2, LAGS, PAIRS, BIN_LOCAL).transpose(2, 1, 0, 3).reshape(PAIRS, LAGS, ROWS)
    same = np.eye(TILE)
    spread = table[:, :, None, :, None] * same[None, None, :, None, :]
    return spread.reshape(PAIRS, LAGS * TILE, ROWS * TILE).astype(BF16)


def swap_rows():
    index = np.arange(TILE * TILE)
    table = np.zeros((TILE * TILE, TILE * TILE))
    table[index, (index % TILE) * TILE + index // TILE] = 1.0
    return table.astype(BF16)


def kernel(
    records, fourier, lagtab, swap, offsets, sides,
    first, second,
    rec_v, fourier_v, lagtab_v, swap_v,
    shares, spectra, staged, own, far, near, own_t, far_t, cross, lagged, arrived,
    load_sem, table_sem, ys, yr, own_s, own_r, near_s, near_r, far_s, far_r, here_sem, lag_s, lag_r, sec_s, sec_r,
):
    me = lax.axis_index("blk")
    q = lax.axis_index("pair")
    barrier = pltpu.get_barrier_semaphore()

    loads = []
    table_loads = [
        pltpu.make_async_copy(fourier, fourier_v, table_sem.at[0]),
        pltpu.make_async_copy(swap, swap_v, table_sem.at[1]),
        pltpu.make_async_copy(lagtab.at[q], lagtab_v, table_sem.at[2]),
    ]
    table_loads[0].start()
    width = GROUP * BLOCK_CH
    for g in range(GROUPS):
        copy = pltpu.make_async_copy(records.at[0, pl.ds(g * width, width)], rec_v.at[g], load_sem.at[g])
        copy.start()
        loads.append(copy)
    table_loads[1].start()
    table_loads[2].start()

    def greet(t, carry):
        pl.semaphore_signal(barrier, inc=1, device_id=(lax.rem(me + t, BLOCKS), q), device_id_type=MESH)
        return carry

    lax.fori_loop(1, BLOCKS, greet, 0)
    for t in range(1, PAIRS):
        pl.semaphore_signal(barrier, inc=1, device_id=(me, lax.rem(q + t, PAIRS)), device_id_type=MESH)

    def whiten(g):
        out = lax.dot_general(
            fourier_v[...], rec_v[g], (((1,), (1,)), ((), ())), preferred_element_type=F32
        )
        spectrum = (out[: 2 * BINS] + out[2 * BINS :]).reshape(PAIRS, 2, BIN_LOCAL, width)
        power = spectrum[:, 0] * spectrum[:, 0] + spectrum[:, 1] * spectrum[:, 1]
        for i in range(GROUP):
            lanes = slice(i * BLOCK_CH, (i + 1) * BLOCK_CH)
            level = jnp.sum(power[:, :, lanes], axis=-1, keepdims=True) * (1.0 / BLOCK_CH)
            scale = 1.0 / jnp.sqrt(level + 1e-05)
            white = (spectrum[:, :, :, lanes] * scale[:, None]).astype(BF16)
            shares[:, g * GROUP + i] = white.reshape(PAIRS, ROWS, BLOCK_CH)
            spectra[q * LOCAL_BLOCKS + g * GROUP + i] = shares[q, g * GROUP + i]

    def send_block(source, target, b, send_sem, recv_sem):
        @pl.when(b != me)
        def _():
            pltpu.make_async_remote_copy(
                src_ref=source.at[b], dst_ref=target.at[me], send_sem=send_sem, recv_sem=recv_sem,
                device_id=(b, q), device_id_type=MESH,
            ).start()

    def send_group(g):
        for t in range(1, PAIRS):
            peer = lax.rem(q + t, PAIRS)
            pltpu.make_async_remote_copy(
                src_ref=shares.at[peer, pl.ds(g * GROUP, GROUP)],
                dst_ref=spectra.at[pl.ds(q * LOCAL_BLOCKS + g * GROUP, GROUP)],
                send_sem=ys.at[t], recv_sem=yr.at[t],
                device_id=(me, peer), device_id_type=MESH,
            ).start()
        for i in range(GROUP):
            send_block(spectra, own, q * LOCAL_BLOCKS + g * GROUP + i, own_s, own_r)

    table_loads[0].wait()
    loads[0].wait()
    whiten(0)
    pl.semaphore_wait(barrier, BLOCKS - 1 + PAIRS - 1)
    send_group(0)
    for g in range(1, GROUPS):
        loads[g].wait()

    def group_step(g, carry):
        whiten(g)
        send_group(g)
        return carry

    lax.fori_loop(1, GROUPS, group_step, 0)

    sixteen = spectra.at[pl.ds(0, LOCAL_BLOCKS)]
    for t in (1, 3, 2):
        pltpu.make_async_copy(sixteen, sixteen, yr.at[t]).wait()
        base = lax.rem(q + PAIRS - t, PAIRS) * LOCAL_BLOCKS

        def send_quarter(m, carry):
            send_block(spectra, own, base + lax.rem(m + me, LOCAL_BLOCKS), own_s, own_r)
            return carry

        lax.fori_loop(0, LOCAL_BLOCKS, send_quarter, 0)
    own_here = pltpu.make_async_copy(spectra.at[me], own.at[me], here_sem.at[0])
    own_here.start()

    offset = offsets[0]

    def stage(b, carry):
        staged[b] = spectra[jnp.minimum(b + offset, BLOCKS - 1)]
        return carry

    lax.fori_loop(0, BLOCKS, stage, 0)
    near_here = pltpu.make_async_copy(staged.at[me], near.at[me], here_sem.at[1])
    near_here.start()

    def send_staged(t, carry):
        b = lax.rem(me + t, BLOCKS)
        pltpu.make_async_remote_copy(
            src_ref=staged.at[b], dst_ref=near.at[me], send_sem=near_s, recv_sem=near_r,
            device_id=(b, q), device_id_type=MESH,
        ).start()
        return carry

    lax.fori_loop(1, BLOCKS, send_staged, 0)

    others = own.at[pl.ds(0, BLOCKS - 1)]
    table_loads[1].wait()
    table_loads[2].wait()
    own_here.wait()
    pltpu.make_async_copy(others, others, own_r).wait()
    forward = pltpu.make_async_remote_copy(
        src_ref=own, dst_ref=far, send_sem=far_s, recv_sem=far_r,
        device_id=(lax.rem(me + BLOCKS - LAST_OFFSET, BLOCKS), q), device_id_type=MESH,
    )
    forward.start()

    def turn(source, target):
        def step(i, carry):
            s0 = pl.multiple_of(i // 4 * TILE, TILE)
            f0 = pl.multiple_of(i % 4 * TILE, TILE)
            tile = source[pl.ds(s0, TILE), pl.ds(f0, TILE), :].reshape(TILE * TILE, BLOCK_CH)
            turned = jnp.dot(swap_v[...], tile, preferred_element_type=F32).astype(BF16)
            target[pl.ds(f0, TILE), pl.ds(s0, TILE), :] = turned.reshape(TILE, TILE, BLOCK_CH)
            return carry

        lax.fori_loop(0, (SEGMENTS // TILE) * (ROWS // TILE), step, 0)

    turn(own, own_t)

    def correlate(k):
        side = sides[0, k].astype(F32)
        swapped = jnp.full((SEGMENTS, BLOCK_CH), side, F32).astype(BF16)
        straight = jnp.full((SEGMENTS, BLOCK_CH), 1.0 - side, F32).astype(BF16)

        def bin_step(f, carry):
            own_re, own_im = own_t[f], own_t[BIN_LOCAL + f]
            far_re, far_im = far_t[f], far_t[BIN_LOCAL + f]
            src_re = own_re * straight + far_re * swapped
            src_im = own_im * straight + far_im * swapped
            rec_re = far_re * straight + own_re * swapped
            rec_im = far_im * straight + own_im * swapped
            left = jnp.concatenate((src_re, src_im), axis=0)
            right = jnp.concatenate(
                (jnp.concatenate((rec_re, rec_im), axis=0), jnp.concatenate((rec_im, -rec_re), axis=0)), axis=1
            )
            out = lax.dot_general(left, right, (((0,), (0,)), ((), ())), preferred_element_type=F32)
            cross[f] = out[:, :BLOCK_CH].astype(BF16)
            cross[BIN_LOCAL + f] = out[:, BLOCK_CH:].astype(BF16)
            return carry

        lax.fori_loop(0, BIN_LOCAL, bin_step, 0)

        def lag_step(i, carry):
            c0 = pl.multiple_of(i * 2 * TILE, 2 * TILE)
            c1 = pl.multiple_of(i * 2 * TILE + TILE, TILE)
            cols = jnp.concatenate(
                (
                    cross[:, pl.ds(c0, TILE), :].reshape(ROWS * TILE, BLOCK_CH),
                    cross[:, pl.ds(c1, TILE), :].reshape(ROWS * TILE, BLOCK_CH),
                ),
                axis=1,
            )
            out = jnp.dot(lagtab_v[...], cols, preferred_element_type=F32).astype(BF16)
            lagged[k, :, pl.ds(c0, TILE), :] = out[:, :BLOCK_CH].reshape(LAGS, TILE, BLOCK_CH)
            lagged[k, :, pl.ds(c1, TILE), :] = out[:, BLOCK_CH:].reshape(LAGS, TILE, BLOCK_CH)
            return carry

        lax.fori_loop(0, BLOCK_CH // (2 * TILE), lag_step, 0)
        copies = []
        for t in (2, 1, 3):
            peer = lax.rem(q + t, PAIRS)
            copy = pltpu.make_async_remote_copy(
                src_ref=lagged.at[k, pl.ds(peer * LAG_LOCAL, LAG_LOCAL)], dst_ref=arrived.at[k, t],
                send_sem=lag_s.at[k, t], recv_sem=lag_r.at[k, t],
                device_id=(me, peer), device_id_type=MESH,
            )
            copy.start()
            copies.append(copy)
        return copies

    def finish(k, copies, keep):
        for copy in copies:
            copy.wait_recv()
        factor = keep.astype(F32)

        def lag_sum(l, carry):
            total = lagged[k, q * LAG_LOCAL + l].astype(F32)
            for t in range(1, PAIRS):
                total = total + arrived[k, t, l].astype(F32)
            first[k, l] = (total * factor).astype(BF16)
            return carry

        lax.fori_loop(0, LAG_LOCAL, lag_sum, 0)

    forward.wait_recv()
    turn(far, far_t)
    last_copies = correlate(1)

    near_here.wait()
    pltpu.make_async_copy(others, others, near_r).wait()
    turn(near, far_t)
    near_copies = correlate(0)

    finish(1, last_copies, jnp.where(me + LAST_OFFSET < BLOCKS, 1, 0))
    back = pltpu.make_async_remote_copy(
        src_ref=first.at[1], dst_ref=second, send_sem=sec_s, recv_sem=sec_r,
        device_id=(lax.rem(me + LAST_OFFSET, BLOCKS), q), device_id_type=MESH,
    )
    back.start()
    finish(0, near_copies, jnp.where(me + offset < BLOCKS, 1, 0))
    back.wait_recv()

    for t in range(1, PAIRS):
        pltpu.make_async_copy(sixteen, sixteen, ys.at[t]).wait()
    pltpu.make_async_copy(others, others, own_s).wait()
    pltpu.make_async_copy(others, others, near_s).wait()
    forward.wait_send()
    for copy in last_copies + near_copies:
        copy.wait_send()
    back.wait_send()


def correlations(records, offsets, sides):
    any_space = pl.BlockSpec(memory_space=pl.ANY)
    scalars = pl.BlockSpec(memory_space=pltpu.SMEM)
    vmem = pl.BlockSpec(memory_space=pltpu.VMEM)
    whole = (BLOCKS, ROWS, BLOCK_CH)
    dma = pltpu.SemaphoreType.DMA
    return pl.pallas_call(
        kernel,
        name="correlations",
        out_shape=(
            jax.ShapeDtypeStruct((2, LAG_LOCAL, BLOCK_CH, BLOCK_CH), BF16),
            jax.ShapeDtypeStruct((LAG_LOCAL, BLOCK_CH, BLOCK_CH), BF16),
        ),
        in_specs=[any_space] * 4 + [scalars] * 2,
        out_specs=(vmem, vmem),
        scratch_shapes=[
            pltpu.VMEM((GROUPS, GROUP * BLOCK_CH, SAMPLES), BF16),
            pltpu.VMEM((4 * BINS, SAMPLES), BF16),
            pltpu.VMEM((LAGS * TILE, ROWS * TILE), BF16),
            pltpu.VMEM((TILE * TILE, TILE * TILE), BF16),
            pltpu.VMEM((PAIRS, LOCAL_BLOCKS, ROWS, BLOCK_CH), BF16),
            pltpu.VMEM(whole, BF16),
            pltpu.VMEM(whole, BF16),
            pltpu.VMEM(whole, BF16),
            pltpu.VMEM(whole, BF16),
            pltpu.VMEM(whole, BF16),
            pltpu.VMEM((ROWS, SEGMENTS, BLOCK_CH), BF16),
            pltpu.VMEM((ROWS, SEGMENTS, BLOCK_CH), BF16),
            pltpu.VMEM((ROWS, BLOCK_CH, BLOCK_CH), BF16),
            pltpu.VMEM((2, LAGS, BLOCK_CH, BLOCK_CH), BF16),
            pltpu.VMEM((2, PAIRS, LAG_LOCAL, BLOCK_CH, BLOCK_CH), BF16),
            dma((GROUPS,)), dma((3,)), dma((PAIRS,)), dma((PAIRS,)),
            dma, dma, dma, dma, dma, dma, dma((2,)), dma((2, PAIRS)), dma((2, PAIRS)), dma, dma,
        ],
        compiler_params=pltpu.CompilerParams(
            collective_id=0, has_side_effects=True, vmem_limit_bytes=48 * 1024 * 1024
        ),
    )(records, jnp.asarray(fourier_rows()), jnp.asarray(lag_rows()), jnp.asarray(swap_rows()), offsets, sides)


def moved_ahead(steps):
    return lambda value: lax.ppermute(value, "blk", [(b, b + steps) for b in range(BLOCKS - steps)])


def local(records, offsets, sides):
    first, second_last = correlations(records, offsets, sides)
    second_near = lax.switch(offsets[0] - 1, [moved_ahead(steps) for steps in range(1, LAST_OFFSET)], first[0])
    return first[None], jnp.stack((second_near, second_last))[None]


def solution(mesh):
    return jax.shard_map(
        local,
        mesh=mesh,
        in_specs=(P("blk", "pair", None), P(), P("blk", None)),
        out_specs=(P("blk", None, "pair", None, None), P("blk", None, "pair", None, None)),
        check_vma=False,
    )
```

time: 254 us -> 131 us (0.52)
  Pallas kernels: 0 us -> 108 us
  waiting for transfers between devices: 94.7 us -> 7.06 us
  blocking collectives: 48.5 us -> 0 us
  starting transfers between devices: 39.4 us -> 5.6 us
  local copies, waits for them, and re-layouts: 37.1 us -> 4.61 us
  matrix products: 16.4 us -> 0 us
  other arithmetic: 10.5 us -> 1.79 us
    pallas_call x0 -> x1, Pallas kernels: none -> 108 us  [correlations(): pl.pallas_call(kernel, name='correlations', out_shape=(jax.ShapeDtypeStru...]
    ppermute x4 -> x1, waiting for transfers between devices: 69.8 us -> 7.06 us  [moved_ahead(): lax.ppermute(value, 'blk', [(b, b + steps) for b in range(BLOCKS - steps)])]
    all_to_all x2 -> x0, blocking collectives: 48.5 us -> none  [the longest x1 29.1 us: sum_at_owner(): lax.all_to_all(tiles, axis, split_axis=0, concat_axis=0, tiled=True)]
    all_to_all x1 -> x0, waiting for transfers between devices: 24.9 us -> none  [local(): lax.all_to_all(lax.all_to_all(whitened, 'pair', split_axis=1, concat_axis...]
    ppermute x4 -> x1, starting transfers between devices: 27.3 us -> 5.6 us  [moved_ahead(): lax.ppermute(value, 'blk', [(b, b + steps) for b in range(BLOCKS - steps)])]
    dot_general x4 -> x0, matrix products: 16.4 us -> none  [the longest x1 5.99 us: local(): jnp.einsum('sbcn,nfr->bfsrc', traces, table_high, preferred_element_type=...]
    all_to_all x1 -> x0, starting transfers between devices: 12 us -> none  [local(): lax.all_to_all(lax.all_to_all(whitened, 'pair', split_axis=1, concat_axis...]
    another operation x3 -> x0, local copies, waits for them, and re-layouts: 7.48 us -> none  [the longest x2 4.52 us: local(): jnp.stack([lax.switch(offsets[slot] - 1, ahead_list, own_block) for slot...]
  transfers between devices with their start and end apart: 5 -> 1, of which waited for: 5 -> 1; matrix products, arithmetic and copies ran while one was open for 0% -> 0% of each run, Pallas kernels for 0% -> 0%
where the time goes in v1:
time: 131 us; the launch traced here: 128 us
  Pallas kernels  108 us (82%)
  waiting for transfers between devices  7.06 us (5%)
  starting transfers between devices  5.6 us (4%)
  local copies, waits for them, and re-layouts  4.61 us (4%)
  other arithmetic  1.79 us (1%)
  between operations  1.31 us (1%)
    pallas_call x1, Pallas kernels, correlations(): pl.pallas_call(kernel, name='correlations', out_shape=(jax.ShapeDtypeStru...  108 us
    ppermute x1, waiting for transfers between devices, moved_ahead(): lax.ppermute(value, 'blk', [(b, b + steps) for b in range(BLOCKS - steps)])  7.06 us
    ppermute x1, starting transfers between devices, moved_ahead(): lax.ppermute(value, 'blk', [(b, b + steps) for b in range(BLOCKS - steps)])  5.6 us
    unnamed x9, local copies, waits for them, and re-layouts  4.59 us
  transfers between devices with their start and end apart: 1, of which 1 were waited for; matrix products, arithmetic and copies ran while one was open for 0% of the time, Pallas kernels for 0%

profile of v1, /device:TPU:2, one launch (start us, length us, event | category | flops | bytes accessed | tf_op | source)
XLA Modules:
  0.0 128.0 jit_solution(15429054206198828893)
XLA Ops:
  1.3 0.0 copy-start
  1.3 1.6 %copy-done = bf16[512,2048]{1,0:T(8,128)(2,1)S(1)} copy-done((bf16[512,2048]{1,0:T(8,128)(2,1)S(1)}, bf16[512,2048]{1,0:T(8,128)(2,1)}, u32[]{:S(2)}) %copy-start) | copy-done | bytes 2097176
  2.9 0.0 copy-start.1
  2.9 0.9 copy-done.1
  3.8 0.0 copy-start.2
  3.8 0.7 copy-done.2
  4.4 0.0 copy-start.3
  4.4 0.7 copy-done.3
  5.1 107.6 %correlations.1 = (bf16[2,8,128,128]{3,2,1,0:T(8,128)(2,1)S(1)}, bf16[8,128,128]{2,1,0:T(8,128)(2,1)S(1)}) custom-call(bf16[1,2048,2048]{2,1,0:T(8,128)(2,1)} %records.1, bf16[512,2048]{1,0:T(8,128)(2,1)S(1)} %copy-done, bf16[4,512,1024]{2,1,0:T(8,128)(2,1)} %constant.17.clone.lagtab, bf16[256,256]{1,0:T(8,128)(2,1)S(1)} %copy-done.1, s32[2]{0:T(128)S(1)} %copy-done.2, ...), custom_call_target="tpu_custom_call" | custom-call | tf_op jit(solution)/shard_map/correlations/pallas_call | solution.py:302
  112.7 12.7 %conditional.1 = (bf16[1,8,128,128]{3,2,1,0:T(8,128)(2,1)}) conditional(s32[]{:T(128)} %bitcast.15, bf16[8,128,128]{2,1,0:T(8,128)(2,1)S(1)} %slice_bitcast_fusion, bf16[8,128,128]{2,1,0:T(8,128)(2,1)S(1)} %slice_bitcast_fusion, bf16[8,128,128]{2,1,0:T(8,128)(2,1)S(1)} %slice_bitcast_fusion, ...), branch_computations={%region_0.0_spmd, %region_1.0_spmd, %region_2.0_spmd, %region_3.0_... | conditional | bytes 1048624 | solution.py:342
  112.8 5.6 %collective-permute-start.13 = (bf16[8,128,128]{2,1,0:T(8,128)(2,1)S(1)}, bf16[8,128,128]{2,1,0:T(8,128)(2,1)}, u32[]{:S(2)}, u32[]{:S(2)}) collective-permute-start(bf16[8,128,128]{2,1,0:T(8,128)(2,1)S(1)} %param.13), channel_id=1, source_target_pairs={{0,56},{4,60},{8,64},{12,68},{16,72},{20,76},{24,80},{28,84},{32,8... | collective-permute-start | bytes 786440 | tf_op jit(solution)/shard_map/cond/branch_13_fun/ppermute | solution.py:337
  118.4 7.1 %collective-permute-done.13 = bf16[8,128,128]{2,1,0:T(8,128)(2,1)} collective-permute-done((bf16[8,128,128]{2,1,0:T(8,128)(2,1)S(1)}, bf16[8,128,128]{2,1,0:T(8,128)(2,1)}, u32[]{:S(2)}, u32[]{:S(2)}) %collective-permute-start.13) | collective-permute-done | bytes 262176 | tf_op jit(solution)/shard_map/cond/branch_13_fun/ppermute | solution.py:337
  125.4 1.8 %maximum_bitcast_fusion = bf16[1,2,8,128,128]{4,3,2,1,0:T(8,128)(2,1)} fusion(bf16[1,8,128,128]{3,2,1,0:T(8,128)(2,1)S(1)} %bitcast.23, bf16[1,8,128,128]{3,2,1,0:T(8,128)(2,1)} %get-tuple-element.40), kind=kLoop, calls=%fused_computation | loop fusion | flops 262144 | bytes 1048576 | tf_op jit(solution)/shard_map/broadcast_in_dim | solution.py:343
  127.2 0.8 copy.23
  (1 shorter events, 0.0 us)
Async XLA Ops:
  1.3 1.6 %copy-start = (bf16[512,2048]{1,0:T(8,128)(2,1)S(1)}, bf16[512,2048]{1,0:T(8,128)(2,1)}, u32[]{:S(2)}) copy-start(bf16[512,2048]{1,0:T(8,128)(2,1)} %constant.16.clone.fourier) | copy-start | bytes 6291460
  2.9 0.9 copy-start.1
  3.8 0.7 copy-start.2
  4.4 0.7 copy-start.3
  112.8 12.7 %collective-permute-start.13 = (bf16[8,128,128]{2,1,0:T(8,128)(2,1)S(1)}, bf16[8,128,128]{2,1,0:T(8,128)(2,1)}, u32[]{:S(2)}, u32[]{:S(2)}) collective-permute-start(bf16[8,128,128]{2,1,0:T(8,128)(2,1)S(1)} %param.13), channel_id=1, source_target_pairs={{0,56},{4,60},{8,64},{12,68},{16,72},{20,76},{24,80},{28,84},{32,8... | collective-permute-start | bytes 786440 | tf_op jit(solution)/shard_map/cond/branch_13_fun/ppermute | solution.py:337

commit v2 on v1

--- a/solution.py
+++ b/solution.py
@@ -24,6 +24,7 @@
 LOCAL_BLOCKS = BLOCKS // PAIRS
 GROUP = 2
 GROUPS = LOCAL_BLOCKS // GROUP
+BEHIND = 4
 TILE = 16
 BF16 = jnp.bfloat16
 F32 = jnp.float32
@@ -61,11 +62,12 @@
 
 
 def kernel(
-    records, fourier, lagtab, swap, offsets, sides,
+    records, fourier, lagtab, swap, offsets_h, sides_h,
     first, second,
-    rec_v, fourier_v, lagtab_v, swap_v,
-    shares, spectra, staged, own, far, near, own_t, far_t, cross, lagged, arrived,
+    rec_v, fourier_v, lagtab_v, swap_v, offsets, sides,
+    shares, spectra, staged, own, far, near, own_t, far_t, cross, lagged, arrived, middle, onward,
     load_sem, table_sem, ys, yr, own_s, own_r, near_s, near_r, far_s, far_r, here_sem, lag_s, lag_r, sec_s, sec_r,
+    mid_s, mid_r, out_s, out_r,
 ):
     me = lax.axis_index("blk")
     q = lax.axis_index("pair")
@@ -76,15 +78,24 @@
         pltpu.make_async_copy(fourier, fourier_v, table_sem.at[0]),
         pltpu.make_async_copy(swap, swap_v, table_sem.at[1]),
         pltpu.make_async_copy(lagtab.at[q], lagtab_v, table_sem.at[2]),
+        pltpu.make_async_copy(offsets_h, offsets, table_sem.at[3]),
+        pltpu.make_async_copy(sides_h, sides, table_sem.at[4]),
     ]
     table_loads[0].start()
     width = GROUP * BLOCK_CH
+    place = lax.rem(me // 2, GROUPS)
+
+    def turn_of(g):
+        ahead = (g % 2) * ((g + 1) // 2) + (1 - g % 2) * (GROUPS - g // 2)
+        return lax.rem(place + ahead, GROUPS)
+
     for g in range(GROUPS):
-        copy = pltpu.make_async_copy(records.at[0, pl.ds(g * width, width)], rec_v.at[g], load_sem.at[g])
+        row = pl.multiple_of(turn_of(g) * width, width)
+        copy = pltpu.make_async_copy(records.at[0, pl.ds(row, width)], rec_v.at[g], load_sem.at[g])
         copy.start()
         loads.append(copy)
-    table_loads[1].start()
-    table_loads[2].start()
+    for copy in table_loads[1:]:
+        copy.start()
 
     def greet(t, carry):
         pl.semaphore_signal(barrier, inc=1, device_id=(lax.rem(me + t, BLOCKS), q), device_id_type=MESH)
@@ -99,14 +110,15 @@
             fourier_v[...], rec_v[g], (((1,), (1,)), ((), ())), preferred_element_type=F32
         )
         spectrum = (out[: 2 * BINS] + out[2 * BINS :]).reshape(PAIRS, 2, BIN_LOCAL, width)
+        at = turn_of(g) * GROUP
         power = spectrum[:, 0] * spectrum[:, 0] + spectrum[:, 1] * spectrum[:, 1]
         for i in range(GROUP):
             lanes = slice(i * BLOCK_CH, (i + 1) * BLOCK_CH)
             level = jnp.sum(power[:, :, lanes], axis=-1, keepdims=True) * (1.0 / BLOCK_CH)
             scale = 1.0 / jnp.sqrt(level + 1e-05)
             white = (spectrum[:, :, :, lanes] * scale[:, None]).astype(BF16)
-            shares[:, g * GROUP + i] = white.reshape(PAIRS, ROWS, BLOCK_CH)
-            spectra[q * LOCAL_BLOCKS + g * GROUP + i] = shares[q, g * GROUP + i]
+            shares[:, at + i] = white.reshape(PAIRS, ROWS, BLOCK_CH)
+            spectra[q * LOCAL_BLOCKS + at + i] = shares[q, at + i]
 
     def send_block(source, target, b, send_sem, recv_sem):
         @pl.when(b != me)
@@ -117,16 +129,26 @@
             ).start()
 
     def send_group(g):
-        for t in range(1, PAIRS):
+        at = turn_of(g) * GROUP
+        for t in (2, 1, 3):
             peer = lax.rem(q + t, PAIRS)
             pltpu.make_async_remote_copy(
-                src_ref=shares.at[peer, pl.ds(g * GROUP, GROUP)],
-                dst_ref=spectra.at[pl.ds(q * LOCAL_BLOCKS + g * GROUP, GROUP)],
-                send_sem=ys.at[t], recv_sem=yr.at[t],
+                src_ref=shares.at[peer, pl.ds(at, GROUP)],
+                dst_ref=spectra.at[pl.ds(q * LOCAL_BLOCKS + at, GROUP)],
+                send_sem=ys.at[t], recv_sem=yr.at[t, g],
                 device_id=(me, peer), device_id_type=MESH,
             ).start()
         for i in range(GROUP):
-            send_block(spectra, own, q * LOCAL_BLOCKS + g * GROUP + i, own_s, own_r)
+            send_block(spectra, own, q * LOCAL_BLOCKS + at + i, own_s, own_r)
+
+    def pass_on(g):
+        at = turn_of(g) * GROUP
+        two = spectra.at[pl.ds(0, GROUP)]
+        for t in (1, 3, 2):
+            pltpu.make_async_copy(two, two, yr.at[t, g]).wait()
+            base = lax.rem(q + PAIRS - t, PAIRS) * LOCAL_BLOCKS
+            for i in range(GROUP):
+                send_block(spectra, own, base + at + i, own_s, own_r)
 
     table_loads[0].wait()
     loads[0].wait()
@@ -141,22 +163,30 @@
         send_group(g)
         return carry
 
-    lax.fori_loop(1, GROUPS, group_step, 0)
-
+    def late_step(g, carry):
+        whiten(g)
+        send_group(g)
+        pass_on(g - BEHIND)
+        return carry
+
+    def pass_step(g, carry):
+        pass_on(g)
+        return carry
+
+    lax.fori_loop(1, BEHIND, group_step, 0)
+    lax.fori_loop(BEHIND, GROUPS, late_step, 0)
+    lax.fori_loop(GROUPS - BEHIND, GROUPS, pass_step, 0)
     sixteen = spectra.at[pl.ds(0, LOCAL_BLOCKS)]
-    for t in (1, 3, 2):
-        pltpu.make_async_copy(sixteen, sixteen, yr.at[t]).wait()
-        base = lax.rem(q + PAIRS - t, PAIRS) * LOCAL_BLOCKS
-
-        def send_quarter(m, carry):
-            send_block(spectra, own, base + lax.rem(m + me, LOCAL_BLOCKS), own_s, own_r)
-            return carry
-
-        lax.fori_loop(0, LOCAL_BLOCKS, send_quarter, 0)
     own_here = pltpu.make_async_copy(spectra.at[me], own.at[me], here_sem.at[0])
     own_here.start()
 
+    for copy in table_loads[1:]:
+        copy.wait()
     offset = offsets[0]
+
+    def alternate(t):
+        ahead = (t % 2) * ((t + 1) // 2) + (1 - t % 2) * (BLOCKS - t // 2)
+        return lax.rem(me + ahead, BLOCKS)
 
     def stage(b, carry):
         staged[b] = spectra[jnp.minimum(b + offset, BLOCKS - 1)]
@@ -167,7 +197,7 @@
     near_here.start()
 
     def send_staged(t, carry):
-        b = lax.rem(me + t, BLOCKS)
+        b = alternate(t)
         pltpu.make_async_remote_copy(
             src_ref=staged.at[b], dst_ref=near.at[me], send_sem=near_s, recv_sem=near_r,
             device_id=(b, q), device_id_type=MESH,
@@ -177,8 +207,6 @@
     lax.fori_loop(1, BLOCKS, send_staged, 0)
 
     others = own.at[pl.ds(0, BLOCKS - 1)]
-    table_loads[1].wait()
-    table_loads[2].wait()
     own_here.wait()
     pltpu.make_async_copy(others, others, own_r).wait()
     forward = pltpu.make_async_remote_copy(
@@ -265,22 +293,62 @@
 
         lax.fori_loop(0, LAG_LOCAL, lag_sum, 0)
 
-    forward.wait_recv()
-    turn(far, far_t)
-    last_copies = correlate(1)
-
     near_here.wait()
     pltpu.make_async_copy(others, others, near_r).wait()
     turn(near, far_t)
     near_copies = correlate(0)
 
+    forward.wait_recv()
+    turn(far, far_t)
+    last_copies = correlate(1)
+
+    def part(ref, m):
+        return ref.at[0, m // 8, pl.ds(pl.multiple_of(m % 8 * TILE, TILE), TILE)]
+
+    finish(0, near_copies, jnp.where(me + offset < BLOCKS, 1, 0))
+    mid_here = pltpu.make_async_copy(part(first, me), middle.at[me], here_sem.at[2])
+    mid_here.start()
+
+    def send_part(t, carry):
+        m = alternate(t)
+        pltpu.make_async_remote_copy(
+            src_ref=part(first, m), dst_ref=middle.at[me], send_sem=mid_s, recv_sem=mid_r,
+            device_id=(m, q), device_id_type=MESH,
+        ).start()
+        return carry
+
+    lax.fori_loop(1, BLOCKS, send_part, 0)
+
     finish(1, last_copies, jnp.where(me + LAST_OFFSET < BLOCKS, 1, 0))
     back = pltpu.make_async_remote_copy(
-        src_ref=first.at[1], dst_ref=second, send_sem=sec_s, recv_sem=sec_r,
+        src_ref=first.at[1], dst_ref=second.at[1], send_sem=sec_s, recv_sem=sec_r,
         device_id=(lax.rem(me + LAST_OFFSET, BLOCKS), q), device_id_type=MESH,
     )
     back.start()
-    finish(0, near_copies, jnp.where(me + offset < BLOCKS, 1, 0))
+
+    parts = middle.at[pl.ds(0, BLOCKS - 1)]
+    mid_here.wait()
+    pltpu.make_async_copy(parts, parts, mid_r).wait()
+
+    def stage_part(j, carry):
+        onward[j] = middle[lax.rem(j + BLOCKS - offset, BLOCKS)]
+        return carry
+
+    lax.fori_loop(0, BLOCKS, stage_part, 0)
+    out_here = pltpu.make_async_copy(onward.at[me], part(second, me), here_sem.at[3])
+    out_here.start()
+
+    def send_onward(t, carry):
+        j = alternate(t)
+        pltpu.make_async_remote_copy(
+            src_ref=onward.at[j], dst_ref=part(second, me), send_sem=out_s, recv_sem=out_r,
+            device_id=(j, q), device_id_type=MESH,
+        ).start()
+        return carry
+
+    lax.fori_loop(1, BLOCKS, send_onward, 0)
+    out_here.wait()
+    pltpu.make_async_copy(parts, parts, out_r).wait()
     back.wait_recv()
 
     for t in range(1, PAIRS):
@@ -291,11 +359,12 @@
     for copy in last_copies + near_copies:
         copy.wait_send()
     back.wait_send()
+    pltpu.make_async_copy(parts, parts, mid_s).wait()
+    pltpu.make_async_copy(parts, parts, out_s).wait()
 
 
 def correlations(records, offsets, sides):
-    any_space = pl.BlockSpec(memory_space=pl.ANY)
-    scalars = pl.BlockSpec(memory_space=pltpu.SMEM)
+    hbm = pl.BlockSpec(memory_space=pltpu.HBM)
     vmem = pl.BlockSpec(memory_space=pltpu.VMEM)
     whole = (BLOCKS, ROWS, BLOCK_CH)
     dma = pltpu.SemaphoreType.DMA
@@ -304,15 +373,17 @@
         name="correlations",
         out_shape=(
             jax.ShapeDtypeStruct((2, LAG_LOCAL, BLOCK_CH, BLOCK_CH), BF16),
-            jax.ShapeDtypeStruct((LAG_LOCAL, BLOCK_CH, BLOCK_CH), BF16),
+            jax.ShapeDtypeStruct((2, LAG_LOCAL, BLOCK_CH, BLOCK_CH), BF16),
         ),
-        in_specs=[any_space] * 4 + [scalars] * 2,
+        in_specs=[hbm] * 6,
         out_specs=(vmem, vmem),
         scratch_shapes=[
             pltpu.VMEM((GROUPS, GROUP * BLOCK_CH, SAMPLES), BF16),
             pltpu.VMEM((4 * BINS, SAMPLES), BF16),
             pltpu.VMEM((LAGS * TILE, ROWS * TILE), BF16),
             pltpu.VMEM((TILE * TILE, TILE * TILE), BF16),
+            pltpu.SMEM((2,), jnp.int32),
+            pltpu.SMEM((1, 2), jnp.int32),
             pltpu.VMEM((PAIRS, LOCAL_BLOCKS, ROWS, BLOCK_CH), BF16),
             pltpu.VMEM(whole, BF16),
             pltpu.VMEM(whole, BF16),
@@ -324,23 +395,21 @@
             pltpu.VMEM((ROWS, BLOCK_CH, BLOCK_CH), BF16),
             pltpu.VMEM((2, LAGS, BLOCK_CH, BLOCK_CH), BF16),
             pltpu.VMEM((2, PAIRS, LAG_LOCAL, BLOCK_CH, BLOCK_CH), BF16),
-            dma((GROUPS,)), dma((3,)), dma((PAIRS,)), dma((PAIRS,)),
-            dma, dma, dma, dma, dma, dma, dma((2,)), dma((2, PAIRS)), dma((2, PAIRS)), dma, dma,
+            pltpu.VMEM((BLOCKS, TILE, BLOCK_CH), BF16),
+            pltpu.VMEM((BLOCKS, TILE, BLOCK_CH), BF16),
+            dma((GROUPS,)), dma((5,)), dma((PAIRS,)), dma((PAIRS, GROUPS)),
+            dma, dma, dma, dma, dma, dma, dma((4,)), dma((2, PAIRS)), dma((2, PAIRS)), dma, dma,
+            dma, dma, dma, dma,
         ],
         compiler_params=pltpu.CompilerParams(
-            collective_id=0, has_side_effects=True, vmem_limit_bytes=48 * 1024 * 1024
+            collective_id=0, has_side_effects=True, vmem_limit_bytes=62 * 1024 * 1024
         ),
     )(records, jnp.asarray(fourier_rows()), jnp.asarray(lag_rows()), jnp.asarray(swap_rows()), offsets, sides)
 
 
-def moved_ahead(steps):
-    return lambda value: lax.ppermute(value, "blk", [(b, b + steps) for b in range(BLOCKS - steps)])
-
-
 def local(records, offsets, sides):
-    first, second_last = correlations(records, offsets, sides)
-    second_near = lax.switch(offsets[0] - 1, [moved_ahead(steps) for steps in range(1, LAST_OFFSET)], first[0])
-    return first[None], jnp.stack((second_near, second_last))[None]
+    first, second = correlations(records, offsets, sides)
+    return first[None], second[None]
 
 
 def solution(mesh):

time: 131 us -> 120 us (0.916); the launches traced: 128 us -> 119 us
  waiting for transfers between devices: 7.06 us -> 0 us
  Pallas kernels: 108 us -> 114 us
  starting transfers between devices: 5.6 us -> 0 us
  other arithmetic: 1.79 us -> 0 us
    ppermute x1 -> x0, waiting for transfers between devices: 7.06 us -> none  [moved_ahead(): lax.ppermute(value, 'blk', [(b, b + steps) for b in range(BLOCKS - steps)])]
    pallas_call x1, Pallas kernels: 108 us -> 114 us  [correlations(): pl.pallas_call(kernel, name='correlations', out_shape=(jax.ShapeDtypeStru...]
    ppermute x1 -> x0, starting transfers between devices: 5.6 us -> none  [moved_ahead(): lax.ppermute(value, 'blk', [(b, b + steps) for b in range(BLOCKS - steps)])]
    broadcast_in_dim x1 -> x0, other arithmetic: 1.79 us -> none  [local(): return (first[None], jnp.stack((second_near, second_last))[None])]
    unnamed x9 -> x2, local copies, waits for them, and re-layouts: 4.59 us -> 3.77 us
  transfers between devices with their start and end apart: 1 -> 0, of which waited for: 1 -> 0; matrix products, arithmetic and copies ran while one was open for 0% -> 0% of each run, Pallas kernels for 0% -> 0%
where the time goes in v2:
time: 120 us; the launch traced here: 119 us
  Pallas kernels  114 us (95%)
  local copies, waits for them, and re-layouts  3.77 us (3%)
    pallas_call x1, Pallas kernels, correlations(): pl.pallas_call(kernel, name='correlations', out_shape=(jax.ShapeDtypeStru...  114 us
    unnamed x2, local copies, waits for them, and re-layouts  3.77 us

profile of v2, /device:TPU:2, one launch (start us, length us, event | category | flops | bytes accessed | tf_op | source)
XLA Modules:
  0.0 118.8 jit_solution(5363879395774326247)
XLA Ops:
  0.6 114.4 %correlations.1 = (bf16[2,8,128,128]{3,2,1,0:T(8,128)(2,1)}, bf16[2,8,128,128]{3,2,1,0:T(8,128)(2,1)}) custom-call(bf16[1,2048,2048]{2,1,0:T(8,128)(2,1)} %records.1, bf16[512,2048]{1,0:T(8,128)(2,1)} %constant.6.clone.fourier, bf16[4,512,1024]{2,1,0:T(8,128)(2,1)} %constant.7.clone.lagtab, bf16[256,256]{1,0:T(8,128)(2,1)} %constant.8.clone.swap, ...), custom_call_target="tpu_custom_call" | custom-call | tf_op jit(solution)/shard_map/correlations/pallas_call | solution.py:371
  115.0 1.9 %copy.10 = bf16[1,2,8,128,128]{4,3,2,1,0:T(8,128)(2,1)} copy(bf16[1,2,8,128,128]{4,3,2,1,0:T(8,128)(2,1)} %bitcast.3) | data formatting | bytes 1048576
  116.9 1.9 %copy.11 = bf16[1,2,8,128,128]{4,3,2,1,0:T(8,128)(2,1)} copy(bf16[1,2,8,128,128]{4,3,2,1,0:T(8,128)(2,1)} %bitcast.2) | data formatting | bytes 1048576

commit v3 on v2

--- a/solution.py
+++ b/solution.py
@@ -21,6 +21,7 @@
 BIN_LOCAL = BINS // PAIRS
 ROWS = 2 * BIN_LOCAL
 LAG_LOCAL = LAGS // PAIRS
+LAG_HALF = LAG_LOCAL // 2
 LOCAL_BLOCKS = BLOCKS // PAIRS
 GROUP = 2
 GROUPS = LOCAL_BLOCKS // GROUP
@@ -65,7 +66,7 @@
     records, fourier, lagtab, swap, offsets_h, sides_h,
     first, second,
     rec_v, fourier_v, lagtab_v, swap_v, offsets, sides,
-    shares, spectra, staged, own, far, near, own_t, far_t, cross, lagged, arrived, middle, onward,
+    shares, spectra, staged, own, far, near, own_t, far_t, cross, lagged, arrived, middle, onward, sums,
     load_sem, table_sem, ys, yr, own_s, own_r, near_s, near_r, far_s, far_r, here_sem, lag_s, lag_r, sec_s, sec_r,
     mid_s, mid_r, out_s, out_r,
 ):
@@ -209,29 +210,38 @@
     others = own.at[pl.ds(0, BLOCKS - 1)]
     own_here.wait()
     pltpu.make_async_copy(others, others, own_r).wait()
+    down = me % LAST_OFFSET % 2 == 0
+    has_lower = me >= LAST_OFFSET
+    has_upper = me + LAST_OFFSET < BLOCKS
+    lower = lax.rem(me + BLOCKS - LAST_OFFSET, BLOCKS)
+    upper = lax.rem(me + LAST_OFFSET, BLOCKS)
+    gives = (down & has_lower) | (~down & has_upper)
+    works = (down & has_upper) | (~down & has_lower)
+    own[SEGMENTS] = jnp.full((ROWS, BLOCK_CH), sides[0, 1].astype(F32), F32).astype(BF16)
     forward = pltpu.make_async_remote_copy(
         src_ref=own, dst_ref=far, send_sem=far_s, recv_sem=far_r,
-        device_id=(lax.rem(me + BLOCKS - LAST_OFFSET, BLOCKS), q), device_id_type=MESH,
+        device_id=(jnp.where(down, lower, upper), q), device_id_type=MESH,
     )
-    forward.start()
+
+    @pl.when(gives)
+    def _():
+        forward.start()
 
     def turn(source, target):
-        def step(i, carry):
-            s0 = pl.multiple_of(i // 4 * TILE, TILE)
-            f0 = pl.multiple_of(i % 4 * TILE, TILE)
-            tile = source[pl.ds(s0, TILE), pl.ds(f0, TILE), :].reshape(TILE * TILE, BLOCK_CH)
-            turned = jnp.dot(swap_v[...], tile, preferred_element_type=F32).astype(BF16)
-            target[pl.ds(f0, TILE), pl.ds(s0, TILE), :] = turned.reshape(TILE, TILE, BLOCK_CH)
-            return carry
-
-        lax.fori_loop(0, (SEGMENTS // TILE) * (ROWS // TILE), step, 0)
+        for i in range(SEGMENTS // TILE):
+            for j in range(0, ROWS // TILE, 2):
+                segs = slice(i * TILE, (i + 1) * TILE)
+                rows = [slice((j + n) * TILE, (j + n + 1) * TILE) for n in range(2)]
+                tiles = [source[segs, row, :].reshape(TILE * TILE, BLOCK_CH) for row in rows]
+                turned = jnp.dot(swap_v[...], jnp.concatenate(tiles, axis=1), preferred_element_type=F32).astype(BF16)
+                for n in range(2):
+                    lanes = slice(n * BLOCK_CH, (n + 1) * BLOCK_CH)
+                    target[rows[n], segs, :] = turned[:, lanes].reshape(TILE, TILE, BLOCK_CH)
 
     turn(own, own_t)
 
-    def correlate(k):
-        side = sides[0, k].astype(F32)
-        swapped = jnp.full((SEGMENTS, BLOCK_CH), side, F32).astype(BF16)
-        straight = jnp.full((SEGMENTS, BLOCK_CH), 1.0 - side, F32).astype(BF16)
+    def correlate(k, swapped):
+        straight = 1.0 - swapped
 
         def bin_step(f, carry):
             own_re, own_im = own_t[f], own_t[BIN_LOCAL + f]
@@ -249,7 +259,7 @@
             cross[BIN_LOCAL + f] = out[:, BLOCK_CH:].astype(BF16)
             return carry
 
-        lax.fori_loop(0, BIN_LOCAL, bin_step, 0)
+        lax.fori_loop(0, BIN_LOCAL, bin_step, 0, unroll=4)
 
         def lag_step(i, carry):
             c0 = pl.multiple_of(i * 2 * TILE, 2 * TILE)
@@ -266,65 +276,80 @@
             lagged[k, :, pl.ds(c1, TILE), :] = out[:, BLOCK_CH:].reshape(LAGS, TILE, BLOCK_CH)
             return carry
 
-        lax.fori_loop(0, BLOCK_CH // (2 * TILE), lag_step, 0)
+        lax.fori_loop(0, BLOCK_CH // (2 * TILE), lag_step, 0, unroll=4)
         copies = []
-        for t in (2, 1, 3):
-            peer = lax.rem(q + t, PAIRS)
-            copy = pltpu.make_async_remote_copy(
-                src_ref=lagged.at[k, pl.ds(peer * LAG_LOCAL, LAG_LOCAL)], dst_ref=arrived.at[k, t],
-                send_sem=lag_s.at[k, t], recv_sem=lag_r.at[k, t],
-                device_id=(me, peer), device_id_type=MESH,
-            )
-            copy.start()
-            copies.append(copy)
+        for h in range(2):
+            for t in (2, 1, 3):
+                peer = lax.rem(q + t, PAIRS)
+                copy = pltpu.make_async_remote_copy(
+                    src_ref=lagged.at[k, pl.ds(peer * LAG_LOCAL + h * LAG_HALF, LAG_HALF)],
+                    dst_ref=arrived.at[k, t, pl.ds(h * LAG_HALF, LAG_HALF)],
+                    send_sem=lag_s.at[k, t, h], recv_sem=lag_r.at[k, t, h],
+                    device_id=(me, peer), device_id_type=MESH,
+                )
+                copy.start()
+                copies.append(copy)
         return copies
 
-    def finish(k, copies, keep):
-        for copy in copies:
+    def lag_sums(k, h, copies, put):
+        for copy in copies[h * (PAIRS - 1) : (h + 1) * (PAIRS - 1)]:
             copy.wait_recv()
-        factor = keep.astype(F32)
 
         def lag_sum(l, carry):
             total = lagged[k, q * LAG_LOCAL + l].astype(F32)
             for t in range(1, PAIRS):
                 total = total + arrived[k, t, l].astype(F32)
-            first[k, l] = (total * factor).astype(BF16)
+            put(l, total)
             return carry
 
-        lax.fori_loop(0, LAG_LOCAL, lag_sum, 0)
+        lax.fori_loop(h * LAG_HALF, (h + 1) * LAG_HALF, lag_sum, 0)
 
     near_here.wait()
     pltpu.make_async_copy(others, others, near_r).wait()
     turn(near, far_t)
-    near_copies = correlate(0)
-
-    forward.wait_recv()
+    near_copies = correlate(0, jnp.full((SEGMENTS, BLOCK_CH), sides[0, 0].astype(F32), F32).astype(BF16))
+
+    @pl.when(works)
+    def _():
+        forward.wait_recv()
+
+    @pl.when(~works)
+    def _():
+        far[...] = jnp.zeros_like(far)
+
     turn(far, far_t)
-    last_copies = correlate(1)
+    is_down = jnp.full((SEGMENTS, BLOCK_CH), jnp.where(down, 1, 0).astype(F32), F32).astype(BF16)
+    last_copies = correlate(1, is_down * own[SEGMENTS] + (1.0 - is_down) * (1.0 - far[SEGMENTS]))
 
     def part(ref, m):
-        return ref.at[0, m // 8, pl.ds(pl.multiple_of(m % 8 * TILE, TILE), TILE)]
-
-    finish(0, near_copies, jnp.where(me + offset < BLOCKS, 1, 0))
+        n = m // 2
+        lag = m % 2 * LAG_HALF + n // 8
+        return ref.at[0, lag, pl.ds(pl.multiple_of(n % 8 * TILE, TILE), TILE)]
+
+    keep = jnp.where(me + offset < BLOCKS, 1, 0).astype(F32)
+
+    def put_near(l, total):
+        first[0, l] = (total * keep).astype(BF16)
+
+    for h in range(2):
+        lag_sums(0, h, near_copies, put_near)
+
+        def send_part(t, carry):
+            ahead = (t % 2) * ((t + 1) // 2) + (1 - t % 2) * (BLOCKS // 2 - t // 2)
+            m = lax.rem(me // 2 + ahead, BLOCKS // 2) * 2 + h
+
+            @pl.when(m != me)
+            def _():
+                pltpu.make_async_remote_copy(
+                    src_ref=part(first, m), dst_ref=middle.at[me], send_sem=mid_s, recv_sem=mid_r,
+                    device_id=(m, q), device_id_type=MESH,
+                ).start()
+
+            return carry
+
+        lax.fori_loop(0, BLOCKS // 2, send_part, 0)
     mid_here = pltpu.make_async_copy(part(first, me), middle.at[me], here_sem.at[2])
     mid_here.start()
-
-    def send_part(t, carry):
-        m = alternate(t)
-        pltpu.make_async_remote_copy(
-            src_ref=part(first, m), dst_ref=middle.at[me], send_sem=mid_s, recv_sem=mid_r,
-            device_id=(m, q), device_id_type=MESH,
-        ).start()
-        return carry
-
-    lax.fori_loop(1, BLOCKS, send_part, 0)
-
-    finish(1, last_copies, jnp.where(me + LAST_OFFSET < BLOCKS, 1, 0))
-    back = pltpu.make_async_remote_copy(
-        src_ref=first.at[1], dst_ref=second.at[1], send_sem=sec_s, recv_sem=sec_r,
-        device_id=(lax.rem(me + LAST_OFFSET, BLOCKS), q), device_id_type=MESH,
-    )
-    back.start()
 
     parts = middle.at[pl.ds(0, BLOCKS - 1)]
     mid_here.wait()
@@ -347,18 +372,65 @@
         return carry
 
     lax.fori_loop(1, BLOCKS, send_onward, 0)
+    def put_last(l, total):
+        sums[l] = total.astype(BF16)
+
+    for h in range(2):
+        lag_sums(1, h, last_copies, put_last)
+
+    def hand_over(target, device):
+        return pltpu.make_async_remote_copy(
+            src_ref=sums, dst_ref=target.at[1], send_sem=sec_s, recv_sem=sec_r,
+            device_id=(device, q), device_id_type=MESH,
+        )
+
+    @pl.when(down & has_upper)
+    def _():
+        hand_over(second, upper).start()
+
+    @pl.when(~down & has_lower)
+    def _():
+        hand_over(first, lower).start()
+
+    @pl.when(down)
+    def _():
+        first[1] = sums[...]
+
+    @pl.when(~down)
+    def _():
+        second[1] = sums[...]
+
+    @pl.when(down & ~has_lower)
+    def _():
+        second[1] = jnp.zeros_like(sums)
+
+    @pl.when(~down & ~has_upper)
+    def _():
+        first[1] = jnp.zeros_like(sums)
+
     out_here.wait()
     pltpu.make_async_copy(parts, parts, out_r).wait()
-    back.wait_recv()
+
+    @pl.when(gives)
+    def _():
+        pltpu.make_async_copy(sums, sums, sec_r).wait()
 
     for t in range(1, PAIRS):
         pltpu.make_async_copy(sixteen, sixteen, ys.at[t]).wait()
     pltpu.make_async_copy(others, others, own_s).wait()
     pltpu.make_async_copy(others, others, near_s).wait()
-    forward.wait_send()
+
+    @pl.when(gives)
+    def _():
+        forward.wait_send()
+
     for copy in last_copies + near_copies:
         copy.wait_send()
-    back.wait_send()
+
+    @pl.when(works)
+    def _():
+        pltpu.make_async_copy(sums, sums, sec_s).wait()
+
     pltpu.make_async_copy(parts, parts, mid_s).wait()
     pltpu.make_async_copy(parts, parts, out_s).wait()
 
@@ -367,6 +439,7 @@
     hbm = pl.BlockSpec(memory_space=pltpu.HBM)
     vmem = pl.BlockSpec(memory_space=pltpu.VMEM)
     whole = (BLOCKS, ROWS, BLOCK_CH)
+    more = (SEGMENTS + 1, ROWS, BLOCK_CH)
     dma = pltpu.SemaphoreType.DMA
     return pl.pallas_call(
         kernel,
@@ -387,8 +460,8 @@
             pltpu.VMEM((PAIRS, LOCAL_BLOCKS, ROWS, BLOCK_CH), BF16),
             pltpu.VMEM(whole, BF16),
             pltpu.VMEM(whole, BF16),
-            pltpu.VMEM(whole, BF16),
-            pltpu.VMEM(whole, BF16),
+            pltpu.VMEM(more, BF16),
+            pltpu.VMEM(more, BF16),
             pltpu.VMEM(whole, BF16),
             pltpu.VMEM((ROWS, SEGMENTS, BLOCK_CH), BF16),
             pltpu.VMEM((ROWS, SEGMENTS, BLOCK_CH), BF16),
@@ -397,8 +470,9 @@
             pltpu.VMEM((2, PAIRS, LAG_LOCAL, BLOCK_CH, BLOCK_CH), BF16),
             pltpu.VMEM((BLOCKS, TILE, BLOCK_CH), BF16),
             pltpu.VMEM((BLOCKS, TILE, BLOCK_CH), BF16),
+            pltpu.VMEM((LAG_LOCAL, BLOCK_CH, BLOCK_CH), BF16),
             dma((GROUPS,)), dma((5,)), dma((PAIRS,)), dma((PAIRS, GROUPS)),
-            dma, dma, dma, dma, dma, dma, dma((4,)), dma((2, PAIRS)), dma((2, PAIRS)), dma, dma,
+            dma, dma, dma, dma, dma, dma, dma((4,)), dma((2, PAIRS, 2)), dma((2, PAIRS, 2)), dma, dma,
             dma, dma, dma, dma,
         ],
         compiler_params=pltpu.CompilerParams(

time: 120 us -> 105 us (0.88)
  Pallas kernels: 114 us -> 99.1 us
    pallas_call x1, Pallas kernels: 114 us -> 99.1 us  [correlations(): pl.pallas_call(kernel, name='correlations', out_shape=(jax.ShapeDtypeStru...]
where the time goes in v3:
time: 105 us; the launch traced here: 103 us
  Pallas kernels  99.1 us (94%)
  local copies, waits for them, and re-layouts  3.77 us (4%)
    pallas_call x1, Pallas kernels, correlations(): pl.pallas_call(kernel, name='correlations', out_shape=(jax.ShapeDtypeStru...  99.1 us
    unnamed x2, local copies, waits for them, and re-layouts  3.77 us

profile of v3, /device:TPU:2, one launch (start us, length us, event | category | flops | bytes accessed | tf_op | source)
XLA Modules:
  0.0 103.5 jit_solution(8281221200503177578)
XLA Ops:
  0.6 99.1 %correlations.1 = (bf16[2,8,128,128]{3,2,1,0:T(8,128)(2,1)}, bf16[2,8,128,128]{3,2,1,0:T(8,128)(2,1)}) custom-call(bf16[1,2048,2048]{2,1,0:T(8,128)(2,1)} %records.1, bf16[512,2048]{1,0:T(8,128)(2,1)} %constant.6.clone.fourier, bf16[4,512,1024]{2,1,0:T(8,128)(2,1)} %constant.7.clone.lagtab, bf16[256,256]{1,0:T(8,128)(2,1)} %constant.8.clone.swap, ...), custom_call_target="tpu_custom_call" | custom-call | tf_op jit(solution)/shard_map/correlations/pallas_call | solution.py:444
  99.7 1.9 %copy.10 = bf16[1,2,8,128,128]{4,3,2,1,0:T(8,128)(2,1)} copy(bf16[1,2,8,128,128]{4,3,2,1,0:T(8,128)(2,1)} %bitcast.3) | data formatting | bytes 1048576
  101.6 1.9 %copy.11 = bf16[1,2,8,128,128]{4,3,2,1,0:T(8,128)(2,1)} copy(bf16[1,2,8,128,128]{4,3,2,1,0:T(8,128)(2,1)} %bitcast.2) | data formatting | bytes 1048576

commit v4 on v3

--- a/solution.py
+++ b/solution.py
@@ -66,7 +66,7 @@
     records, fourier, lagtab, swap, offsets_h, sides_h,
     first, second,
     rec_v, fourier_v, lagtab_v, swap_v, offsets, sides,
-    shares, spectra, staged, own, far, near, own_t, far_t, cross, lagged, arrived, middle, onward, sums,
+    shares, spectra, staged, own, far, near, own_t, far_t, cross, lagged, arrived, middle, onward, outgoing, sums,
     load_sem, table_sem, ys, yr, own_s, own_r, near_s, near_r, far_s, far_r, here_sem, lag_s, lag_r, sec_s, sec_r,
     mid_s, mid_r, out_s, out_r,
 ):
@@ -98,11 +98,23 @@
     for copy in table_loads[1:]:
         copy.start()
 
-    def greet(t, carry):
-        pl.semaphore_signal(barrier, inc=1, device_id=(lax.rem(me + t, BLOCKS), q), device_id_type=MESH)
-        return carry
-
-    lax.fori_loop(1, BLOCKS, greet, 0)
+    def wrapped(value, count):
+        value = jnp.where(value >= count, value - count, value)
+        return jnp.where(value < 0, value + count, value)
+
+    def both_ways(here, count, send):
+        def step(t, carry):
+            send(wrapped(here + count // 2 - t, count))
+            send(wrapped(here - count // 2 + t, count))
+            return carry
+
+        send(wrapped(here + count // 2, count))
+        lax.fori_loop(1, count // 2, step, 0)
+
+    def greet(b):
+        pl.semaphore_signal(barrier, inc=1, device_id=(b, q), device_id_type=MESH)
+
+    both_ways(me, BLOCKS, greet)
     for t in range(1, PAIRS):
         pl.semaphore_signal(barrier, inc=1, device_id=(me, lax.rem(q + t, PAIRS)), device_id_type=MESH)
 
@@ -185,10 +197,6 @@
         copy.wait()
     offset = offsets[0]
 
-    def alternate(t):
-        ahead = (t % 2) * ((t + 1) // 2) + (1 - t % 2) * (BLOCKS - t // 2)
-        return lax.rem(me + ahead, BLOCKS)
-
     def stage(b, carry):
         staged[b] = spectra[jnp.minimum(b + offset, BLOCKS - 1)]
         return carry
@@ -197,15 +205,13 @@
     near_here = pltpu.make_async_copy(staged.at[me], near.at[me], here_sem.at[1])
     near_here.start()
 
-    def send_staged(t, carry):
-        b = alternate(t)
+    def send_staged(b):
         pltpu.make_async_remote_copy(
             src_ref=staged.at[b], dst_ref=near.at[me], send_sem=near_s, recv_sem=near_r,
             device_id=(b, q), device_id_type=MESH,
         ).start()
-        return carry
-
-    lax.fori_loop(1, BLOCKS, send_staged, 0)
+
+    both_ways(me, BLOCKS, send_staged)
 
     others = own.at[pl.ds(0, BLOCKS - 1)]
     own_here.wait()
@@ -218,14 +224,19 @@
     gives = (down & has_lower) | (~down & has_upper)
     works = (down & has_upper) | (~down & has_lower)
     own[SEGMENTS] = jnp.full((ROWS, BLOCK_CH), sides[0, 1].astype(F32), F32).astype(BF16)
-    forward = pltpu.make_async_remote_copy(
-        src_ref=own, dst_ref=far, send_sem=far_s, recv_sem=far_r,
-        device_id=(jnp.where(down, lower, upper), q), device_id_type=MESH,
-    )
+    receiver = jnp.where(down, lower, upper)
+
+    def forward(start, count):
+        piece = pl.ds(start, count)
+        return pltpu.make_async_remote_copy(
+            src_ref=own.at[piece], dst_ref=far.at[piece], send_sem=far_s, recv_sem=far_r,
+            device_id=(receiver, q), device_id_type=MESH,
+        )
 
     @pl.when(gives)
     def _():
-        forward.start()
+        for start, count in ((0, 16), (16, 16), (32, 16), (48, 17)):
+            forward(start, count).start()
 
     def turn(source, target):
         for i in range(SEGMENTS // TILE):
@@ -295,14 +306,11 @@
         for copy in copies[h * (PAIRS - 1) : (h + 1) * (PAIRS - 1)]:
             copy.wait_recv()
 
-        def lag_sum(l, carry):
+        for l in range(h * LAG_HALF, (h + 1) * LAG_HALF):
             total = lagged[k, q * LAG_LOCAL + l].astype(F32)
             for t in range(1, PAIRS):
                 total = total + arrived[k, t, l].astype(F32)
             put(l, total)
-            return carry
-
-        lax.fori_loop(h * LAG_HALF, (h + 1) * LAG_HALF, lag_sum, 0)
 
     near_here.wait()
     pltpu.make_async_copy(others, others, near_r).wait()
@@ -311,7 +319,7 @@
 
     @pl.when(works)
     def _():
-        forward.wait_recv()
+        pltpu.make_async_copy(far, far, far_r).wait()
 
     @pl.when(~works)
     def _():
@@ -321,34 +329,32 @@
     is_down = jnp.full((SEGMENTS, BLOCK_CH), jnp.where(down, 1, 0).astype(F32), F32).astype(BF16)
     last_copies = correlate(1, is_down * own[SEGMENTS] + (1.0 - is_down) * (1.0 - far[SEGMENTS]))
 
-    def part(ref, m):
-        n = m // 2
-        lag = m % 2 * LAG_HALF + n // 8
-        return ref.at[0, lag, pl.ds(pl.multiple_of(n % 8 * TILE, TILE), TILE)]
-
     keep = jnp.where(me + offset < BLOCKS, 1, 0).astype(F32)
 
+    chip = me // 2
+
     def put_near(l, total):
-        first[0, l] = (total * keep).astype(BF16)
+        value = (total * keep).astype(BF16)
+        first[0, l] = value
+        for r in range(BLOCK_CH // TILE):
+            m = 2 * (l % LAG_HALF * (BLOCK_CH // TILE) + r) + l // LAG_HALF
+            outgoing[m] = value[r * TILE : (r + 1) * TILE]
 
     for h in range(2):
         lag_sums(0, h, near_copies, put_near)
 
-        def send_part(t, carry):
-            ahead = (t % 2) * ((t + 1) // 2) + (1 - t % 2) * (BLOCKS // 2 - t // 2)
-            m = lax.rem(me // 2 + ahead, BLOCKS // 2) * 2 + h
-
-            @pl.when(m != me)
-            def _():
-                pltpu.make_async_remote_copy(
-                    src_ref=part(first, m), dst_ref=middle.at[me], send_sem=mid_s, recv_sem=mid_r,
-                    device_id=(m, q), device_id_type=MESH,
-                ).start()
-
-            return carry
-
-        lax.fori_loop(0, BLOCKS // 2, send_part, 0)
-    mid_here = pltpu.make_async_copy(part(first, me), middle.at[me], here_sem.at[2])
+        def send_part(m):
+            pltpu.make_async_remote_copy(
+                src_ref=outgoing.at[m], dst_ref=middle.at[me], send_sem=mid_s, recv_sem=mid_r,
+                device_id=(m, q), device_id_type=MESH,
+            ).start()
+
+        @pl.when(2 * chip + h != me)
+        def _():
+            send_part(2 * chip + h)
+
+        both_ways(chip, BLOCKS // 2, lambda n: send_part(2 * n + h))
+    mid_here = pltpu.make_async_copy(outgoing.at[me], middle.at[me], here_sem.at[2])
     mid_here.start()
 
     parts = middle.at[pl.ds(0, BLOCKS - 1)]
@@ -356,41 +362,43 @@
     pltpu.make_async_copy(parts, parts, mid_r).wait()
 
     def stage_part(j, carry):
-        onward[j] = middle[lax.rem(j + BLOCKS - offset, BLOCKS)]
+        onward[j] = middle[wrapped(j - offset, BLOCKS)]
         return carry
 
     lax.fori_loop(0, BLOCKS, stage_part, 0)
-    out_here = pltpu.make_async_copy(onward.at[me], part(second, me), here_sem.at[3])
+    spot = second.at[
+        0, me % 2 * LAG_HALF + me // 2 // 8, pl.ds(pl.multiple_of(me // 2 % 8 * TILE, TILE), TILE)
+    ]
+    out_here = pltpu.make_async_copy(onward.at[me], spot, here_sem.at[3])
     out_here.start()
 
-    def send_onward(t, carry):
-        j = alternate(t)
+    def send_onward(j):
         pltpu.make_async_remote_copy(
-            src_ref=onward.at[j], dst_ref=part(second, me), send_sem=out_s, recv_sem=out_r,
+            src_ref=onward.at[j], dst_ref=spot, send_sem=out_s, recv_sem=out_r,
             device_id=(j, q), device_id_type=MESH,
         ).start()
-        return carry
-
-    lax.fori_loop(1, BLOCKS, send_onward, 0)
+
+    both_ways(me, BLOCKS, send_onward)
     def put_last(l, total):
         sums[l] = total.astype(BF16)
 
+    def hand_over(target, device, h):
+        half = pl.ds(h * LAG_HALF, LAG_HALF)
+        return pltpu.make_async_remote_copy(
+            src_ref=sums.at[half], dst_ref=target.at[1, half], send_sem=sec_s, recv_sem=sec_r,
+            device_id=(device, q), device_id_type=MESH,
+        )
+
     for h in range(2):
         lag_sums(1, h, last_copies, put_last)
 
-    def hand_over(target, device):
-        return pltpu.make_async_remote_copy(
-            src_ref=sums, dst_ref=target.at[1], send_sem=sec_s, recv_sem=sec_r,
-            device_id=(device, q), device_id_type=MESH,
-        )
-
-    @pl.when(down & has_upper)
-    def _():
-        hand_over(second, upper).start()
-
-    @pl.when(~down & has_lower)
-    def _():
-        hand_over(first, lower).start()
+        @pl.when(down & has_upper)
+        def _():
+            hand_over(second, upper, h).start()
+
+        @pl.when(~down & has_lower)
+        def _():
+            hand_over(first, lower, h).start()
 
     @pl.when(down)
     def _():
@@ -422,7 +430,7 @@
 
     @pl.when(gives)
     def _():
-        forward.wait_send()
+        pltpu.make_async_copy(own, own, far_s).wait()
 
     for copy in last_copies + near_copies:
         copy.wait_send()
@@ -470,6 +478,7 @@
             pltpu.VMEM((2, PAIRS, LAG_LOCAL, BLOCK_CH, BLOCK_CH), BF16),
             pltpu.VMEM((BLOCKS, TILE, BLOCK_CH), BF16),
             pltpu.VMEM((BLOCKS, TILE, BLOCK_CH), BF16),
+            pltpu.VMEM((BLOCKS, TILE, BLOCK_CH), BF16),
             pltpu.VMEM((LAG_LOCAL, BLOCK_CH, BLOCK_CH), BF16),
             dma((GROUPS,)), dma((5,)), dma((PAIRS,)), dma((PAIRS, GROUPS)),
             dma, dma, dma, dma, dma, dma, dma((4,)), dma((2, PAIRS, 2)), dma((2, PAIRS, 2)), dma, dma,

time: 105 us -> 102 us (0.971)
  Pallas kernels: 99.1 us -> 96.9 us
    pallas_call x1, Pallas kernels: 99.1 us -> 96.9 us  [correlations(): pl.pallas_call(kernel, name='correlations', out_shape=(jax.ShapeDtypeStru...]
where the time goes in v4:
time: 102 us; the launch traced here: 101 us
  Pallas kernels  96.9 us (95%)
  local copies, waits for them, and re-layouts  3.77 us (4%)
    pallas_call x1, Pallas kernels, correlations(): pl.pallas_call(kernel, name='correlations', out_shape=(jax.ShapeDtypeStru...  96.9 us
    unnamed x2, local copies, waits for them, and re-layouts  3.77 us

profile of v4, /device:TPU:2, one launch (start us, length us, event | category | flops | bytes accessed | tf_op | source)
XLA Modules:
  0.0 101.4 jit_solution(9017674895802257256)
XLA Ops:
  0.6 96.9 %correlations.1 = (bf16[2,8,128,128]{3,2,1,0:T(8,128)(2,1)}, bf16[2,8,128,128]{3,2,1,0:T(8,128)(2,1)}) custom-call(bf16[1,2048,2048]{2,1,0:T(8,128)(2,1)} %records.1, bf16[512,2048]{1,0:T(8,128)(2,1)} %constant.6.clone.fourier, bf16[4,512,1024]{2,1,0:T(8,128)(2,1)} %constant.7.clone.lagtab, bf16[256,256]{1,0:T(8,128)(2,1)} %constant.8.clone.swap, ...), custom_call_target="tpu_custom_call" | custom-call | tf_op jit(solution)/shard_map/correlations/pallas_call | solution.py:452
  97.6 1.9 %copy.10 = bf16[1,2,8,128,128]{4,3,2,1,0:T(8,128)(2,1)} copy(bf16[1,2,8,128,128]{4,3,2,1,0:T(8,128)(2,1)} %bitcast.3) | data formatting | bytes 1048576
  99.5 1.9 %copy.11 = bf16[1,2,8,128,128]{4,3,2,1,0:T(8,128)(2,1)} copy(bf16[1,2,8,128,128]{4,3,2,1,0:T(8,128)(2,1)} %bitcast.2) | data formatting | bytes 1048576

commit v5 on v4

--- a/solution.py
+++ b/solution.py
@@ -88,7 +88,7 @@
 
     def turn_of(g):
         ahead = (g % 2) * ((g + 1) // 2) + (1 - g % 2) * (GROUPS - g // 2)
-        return lax.rem(place + ahead, GROUPS)
+        return lax.rem(place + GROUPS // 2 + ahead, GROUPS)
 
     for g in range(GROUPS):
         row = pl.multiple_of(turn_of(g) * width, width)

time: 102 us -> 101 us (level)
  no operation moved by 1% of the time
where the time goes in v5:
time: 101 us
  Pallas kernels  96.3 us (95%)
  local copies, waits for them, and re-layouts  3.77 us (4%)
    pallas_call x1, Pallas kernels, correlations(): pl.pallas_call(kernel, name='correlations', out_shape=(jax.ShapeDtypeStru...  96.3 us
    unnamed x2, local copies, waits for them, and re-layouts  3.77 us

profile of v5, /device:TPU:2, one launch (start us, length us, event | category | flops | bytes accessed | tf_op | source)
XLA Modules:
  0.0 100.7 jit_solution(14690704552672606200)
XLA Ops:
  0.6 96.3 %correlations.1 = (bf16[2,8,128,128]{3,2,1,0:T(8,128)(2,1)}, bf16[2,8,128,128]{3,2,1,0:T(8,128)(2,1)}) custom-call(bf16[1,2048,2048]{2,1,0:T(8,128)(2,1)} %records.1, bf16[512,2048]{1,0:T(8,128)(2,1)} %constant.6.clone.fourier, bf16[4,512,1024]{2,1,0:T(8,128)(2,1)} %constant.7.clone.lagtab, bf16[256,256]{1,0:T(8,128)(2,1)} %constant.8.clone.swap, ...), custom_call_target="tpu_custom_call" | custom-call | tf_op jit(solution)/shard_map/correlations/pallas_call | solution.py:452
  96.9 1.9 %copy.10 = bf16[1,2,8,128,128]{4,3,2,1,0:T(8,128)(2,1)} copy(bf16[1,2,8,128,128]{4,3,2,1,0:T(8,128)(2,1)} %bitcast.3) | data formatting | bytes 1048576
  98.8 1.9 %copy.11 = bf16[1,2,8,128,128]{4,3,2,1,0:T(8,128)(2,1)} copy(bf16[1,2,8,128,128]{4,3,2,1,0:T(8,128)(2,1)} %bitcast.2) | data formatting | bytes 1048576

commit v6 on v5

--- a/solution.py
+++ b/solution.py
@@ -25,7 +25,7 @@
 LOCAL_BLOCKS = BLOCKS // PAIRS
 GROUP = 2
 GROUPS = LOCAL_BLOCKS // GROUP
-BEHIND = 4
+BEHIND = 6
 TILE = 16
 BF16 = jnp.bfloat16
 F32 = jnp.float32

time: 101 us -> 102 us (level)
  no operation moved by 1% of the time
where the time goes in v6:
time: 102 us; the launch traced here: 101 us
  Pallas kernels  97 us (95%)
  local copies, waits for them, and re-layouts  3.77 us (4%)
    pallas_call x1, Pallas kernels, correlations(): pl.pallas_call(kernel, name='correlations', out_shape=(jax.ShapeDtypeStru...  97 us
    unnamed x2, local copies, waits for them, and re-layouts  3.77 us

profile of v6, /device:TPU:2, one launch (start us, length us, event | category | flops | bytes accessed | tf_op | source)
XLA Modules:
  0.0 101.4 jit_solution(11460373233794023270)
XLA Ops:
  0.6 97.0 %correlations.1 = (bf16[2,8,128,128]{3,2,1,0:T(8,128)(2,1)}, bf16[2,8,128,128]{3,2,1,0:T(8,128)(2,1)}) custom-call(bf16[1,2048,2048]{2,1,0:T(8,128)(2,1)} %records.1, bf16[512,2048]{1,0:T(8,128)(2,1)} %constant.6.clone.fourier, bf16[4,512,1024]{2,1,0:T(8,128)(2,1)} %constant.7.clone.lagtab, bf16[256,256]{1,0:T(8,128)(2,1)} %constant.8.clone.swap, ...), custom_call_target="tpu_custom_call" | custom-call | tf_op jit(solution)/shard_map/correlations/pallas_call | solution.py:452
  97.6 1.9 %copy.10 = bf16[1,2,8,128,128]{4,3,2,1,0:T(8,128)(2,1)} copy(bf16[1,2,8,128,128]{4,3,2,1,0:T(8,128)(2,1)} %bitcast.3) | data formatting | bytes 1048576
  99.5 1.9 %copy.11 = bf16[1,2,8,128,128]{4,3,2,1,0:T(8,128)(2,1)} copy(bf16[1,2,8,128,128]{4,3,2,1,0:T(8,128)(2,1)} %bitcast.2) | data formatting | bytes 1048576
